TPU v7x, 128 devices: a whole 4x4x4 slice. The times are simulated.
128 devices in a mesh: dp: 16 (over z, y_lo, core), tensor: 8 (over y_hi, x).
Axes of the slice: x: 4, y: 4 (y_hi: 2, y_lo: 2; y = y_hi * 2 + y_lo), z: 4, core: 2. Of those that a mesh axis runs over, the one named last changes fastest.
Arguments:
- tokens: bfloat16 [16384, 2048], P(('dp', 'tensor')), may hold values from -6 to 6
- cotangent: bfloat16 [16384, 2048], P(('dp', 'tensor')), may hold values from -6 to 6
- doc_lengths: int32 [16, 4], P('dp'), may hold values from 1 to 1021, as said below
- query_weight: float32 [2048, 2048], P('dp', 'tensor'), may hold values from -0.125 to 0.125
- key_value_weight: float32 [2, 2048, 1024], P(None, 'dp', 'tensor'), may hold values from -0.125 to 0.125
- output_weight: float32 [2048, 2048], P('tensor', 'dp'), may hold values from -1.5 to 1.5
- gateup_weight: float32 [2, 2048, 6144], P(None, 'dp', 'tensor'), may hold values from -0.125 to 0.125
- down_weight: float32 [6144, 2048], P('tensor', 'dp'), may hold values from -0.078125 to 0.078125
- norm_gains: float32 [4352], P(('dp', 'tensor')), may hold values from 0.5 to 1.5
- query_momentum: float32 [2048, 2048], P('dp', 'tensor')
- keyval_momentum: float32 [2, 2048, 1024], P(None, 'dp', 'tensor')
- output_momentum: float32 [2048, 2048], P('tensor', 'dp')
- gateup_momentum: float32 [2, 2048, 6144], P(None, 'dp', 'tensor')
- down_momentum: float32 [6144, 2048], P('tensor', 'dp')
- gains_momentum: float32 [4352], P(('dp', 'tensor'))
- query_average: float32 [2048, 2048], P('dp', 'tensor'), may hold values from -0.125 to 0.125
- key_value_mean: float32 [2, 2048, 1024], P(None, 'dp', 'tensor'), may hold values from -0.125 to 0.125
- output_average: float32 [2048, 2048], P('tensor', 'dp'), may hold values from -1.5 to 1.5
- gateup_average: float32 [2, 2048, 6144], P(None, 'dp', 'tensor'), may hold values from -0.125 to 0.125
- down_average: float32 [6144, 2048], P('tensor', 'dp'), may hold values from -0.078125 to 0.078125
- gains_average: float32 [4352], P(('dp', 'tensor')), may hold values from 0.2 to 1.8
Outputs:
- block_out: bfloat16 [16384, 2048], P(('dp', 'tensor'))
- input_grad: bfloat16 [16384, 2048], P(('dp', 'tensor'))
- query_updated: float32 [2048, 2048], P('dp', 'tensor')
- keyval_updated: float32 [2, 2048, 1024], P(None, 'dp', 'tensor')
- output_updated: float32 [2048, 2048], P('tensor', 'dp')
- gateup_updated: float32 [2, 2048, 6144], P(None, 'dp', 'tensor')
- down_updated: float32 [6144, 2048], P('tensor', 'dp')
- gains_updated: float32 [4352], P(('dp', 'tensor'))
- query_velocity: float32 [2048, 2048], P('dp', 'tensor')
- keyval_velocity: float32 [2, 2048, 1024], P(None, 'dp', 'tensor')
- output_velocity: float32 [2048, 2048], P('tensor', 'dp')
- gateup_velocity: float32 [2, 2048, 6144], P(None, 'dp', 'tensor')
- down_velocity: float32 [6144, 2048], P('tensor', 'dp')
- gains_velocity: float32 [4352], P(('dp', 'tensor'))
- query_smoothed: float32 [2048, 2048], P('dp', 'tensor')
- keyval_smoothed: float32 [2, 2048, 1024], P(None, 'dp', 'tensor')
- output_smoothed: float32 [2048, 2048], P('tensor', 'dp')
- gateup_smoothed: float32 [2, 2048, 6144], P(None, 'dp', 'tensor')
- down_smoothed: float32 [6144, 2048], P('tensor', 'dp')
- gains_smoothed: float32 [4352], P(('dp', 'tensor'))
Inputs may be any that keep to these rules, and one draw needn't show every extreme that they name: `doc_lengths`: row g holds the lengths of group g's 4 documents in order, summing to 1024; the first, third and fourth are each at least 1 and under 1024 // 8, the third and fourth together under 1024 // 8.
All inputs are finite; a program needn't handle non-finite values.
Results may differ from a plain program's by a relative error of at most 0.02.
Values may be sent and summed in bfloat16 or wider, within the bound.
A program may use at most 192 MiB of HBM per device.

v0:
```python
import math

import jax
import jax.numpy as jnp
import numpy as np
from jax import lax
from jax.experimental import pallas as pl
from jax.experimental.pallas import tpu as pltpu
from jax.sharding import Mesh
from jax.sharding import PartitionSpec as P

MODEL_WIDTH = 2048
QUERY_HEADS = 16
HEAD_SIZE = 128
FF = 6144
GROUP_TOK = 1024
GAINS = 4352
OWN_GAINS = 34
EPSILON = 1e-06
MOMENTUM = 0.9
AVERAGING = 0.5
ROPE_BASE = 1000000.0
SCALE = HEAD_SIZE ** (-0.5)

AXES = ("z", "ylo", "core", "yhi", "x")
GRID = (4, 2, 2, 2, 4)
RING = 4
BF16 = jnp.bfloat16
F32 = jnp.float32
HBM = pl.ANY
VMEM = pltpu.VMEM


class Place:
    def __init__(self):
        self.x = lax.axis_index("x")
        self.z = lax.axis_index("z")
        self.core = lax.axis_index("core")
        self.yhi = lax.axis_index("yhi")
        self.ylo = lax.axis_index("ylo")
        self.y = self.yhi * 2 + self.ylo
        self.native = self.core == self.yhi
        at = {"x": self.x, "y": self.y, "z": self.z}
        self.steps = {
            (axis, by): lax.rem(here + by, RING) if by else here
            for axis, here in at.items()
            for by in range(RING)
        }
        self.devices = {
            "core": {"core": 1 - self.core},
            "turn": {"core": 1 - self.core, "yhi": 1 - self.yhi},
        }
        for (axis, by), there in self.steps.items():
            self.devices[axis, by] = (
                {"yhi": lax.div(there, 2), "ylo": lax.rem(there, 2)}
                if axis == "y"
                else {axis: there}
            )

    def step(self, axis, by):
        return self.steps[axis, by % RING]

    def device(self, axis, by=1):
        return self.devices[axis] if axis in ("core", "turn") else self.devices[axis, by % RING]


class Local:
    def __init__(self, refs, sems, index):
        self.refs, self.sems, self.index = refs, sems, index

    def copy(self):
        source, target = self.refs()
        return pltpu.make_async_copy(source, target, self.sems.at[self.index])

    def start(self):
        self.copy().start()

    def wait(self):
        self.copy().wait()


class Net:
    def __init__(self, place, partners, send_sems, recv_sems, local_sems):
        self.place, self.partners = place, partners
        self.send_sems, self.recv_sems, self.local_sems = send_sems, recv_sems, local_sems
        self.leaving, self.arriving, self.local_count = 0, 0, 0
        self.waits = []

    def greet(self):
        barrier = pltpu.get_barrier_semaphore()
        for axis, by in self.partners:
            pl.semaphore_signal(
                barrier,
                inc=1,
                device_id=self.place.device(axis, by),
                device_id_type=pl.DeviceIdType.MESH,
            )

    def enter(self):
        pl.semaphore_wait(pltpu.get_barrier_semaphore(), len(self.partners))

    def out(self):
        self.leaving += 1
        return self.leaving - 1

    def into(self):
        self.arriving += 1
        return self.arriving - 1

    def local_number(self):
        self.local_count += 1
        return self.local_count - 1

    def copy(self, source, target, out, into, axis="core", by=1):
        return pltpu.make_async_remote_copy(
            src_ref=source,
            dst_ref=target,
            send_sem=self.send_sems.at[out],
            recv_sem=self.recv_sems.at[into],
            device_id=self.place.device(axis, by),
            device_id_type=pl.DeviceIdType.MESH,
        )

    def send(self, refs, out, into, axis, by=1):
        self.copy(*refs(), out, into, axis, by).start()

    def here(self, into, view):
        self.copy(view, view, 0, into).wait_recv()

    def gone(self, out, view):
        self.copy(view, view, out, 0).wait_send()

    def later(self, wait):
        self.waits.append(wait)

    def finish(self):
        for wait in self.waits:
            wait()

    def local(self, refs):
        copy = Local(refs, self.local_sems, self.local_number())
        copy.start()
        return copy


def staged(count, compute, before=None, after=None):
    def do(acts, n):
        for at, act in (acts or {}).items():

            @pl.when(n == at)
            def _():
                act()

    def step(n, carry):
        do(before, n)
        compute(n)
        do(after, n)
        return carry

    lax.fori_loop(0, count, step, 0)


class RowsGather:
    OUT, INTO, LOCALS = 1, 7, 2

    def __init__(self, net, own, whole):
        self.net, self.own, self.whole = net, own, whole
        self.rows = own.shape[0]
        self.half = self.rows // 2
        place = net.place
        self.me, self.other = place.core, 1 - place.core
        self.spots = {k: place.step("x", k) for k in (0, 1, -1, 2)}
        self.out = net.out()
        self.first, self.second, self.third = net.into(), net.into(), net.into()
        self.shared = {k: net.into() for k in (0, 1, -1, 2)}
        self.kept = []
        net.later(self.gone)

    def block(self, core, k, part):
        start = (self.spots[k] * 2 + core) * self.rows + part * self.half
        return self.whole.at[pl.ds(pl.multiple_of(start, self.half), self.half)]

    def mine(self, k, part):
        return self.block(self.me, k, part)

    def piece(self, part):
        return self.own.at[pl.ds(part * self.half, self.half)]

    def share(self, k, part):
        refs = lambda: (self.piece(part) if k == 0 else self.mine(k, part), self.mine(k, part))
        self.net.send(refs, self.out, self.shared[k], "core")

    def both(self):
        return self.whole.at[pl.ds(0, self.rows)]

    def start(self, parts=(0, 1)):
        for part in parts:
            refs = lambda part=part: (self.piece(part), self.mine(0, part))
            first, second = (1, -1) if part == 0 else (-1, 1)
            self.net.send(refs, self.out, self.first, "x", first)
            self.net.send(refs, self.out, self.second, "x", second)
            self.share(0, part)
            self.kept.append(self.net.local(refs))

    def near_first(self):
        self.net.here(self.first, self.both())
        self.net.send(lambda: (self.mine(-1, 0),) * 2, self.out, self.third, "x", 1)
        self.net.send(lambda: (self.mine(1, 1),) * 2, self.out, self.third, "x", -1)
        self.share(-1, 0)
        self.share(1, 1)

    def near_second(self):
        self.net.here(self.second, self.both())
        self.share(-1, 1)
        self.share(1, 0)

    def far(self):
        self.net.here(self.third, self.both())
        self.share(2, 0)
        self.share(2, 1)

    def here(self, k):
        if k == 0:
            for copy in self.kept:
                copy.wait()
        self.net.here(self.shared[k], self.both())

    def gone(self):
        if self.out is not None:
            self.net.gone(self.out, self.whole.at[pl.ds(0, 7 * self.rows)])
            self.out = None


class RowsSum:
    OUT, INTO = 2, 6

    def __init__(self, net, whole, landed, land):
        self.net, self.whole, self.landed, self.land = net, whole, landed, land
        self.half = landed.shape[2]
        place = net.place
        self.me, self.other = place.core, 1 - place.core
        self.spots = {k: place.step("x", k) for k in (0, 1, -1, 2)}
        self.over, self.along = net.out(), net.out()
        self.given = {k: net.into() for k in (0, 1, -1, 2)}
        self.through, self.last = net.into(), net.into()
        net.later(self.passed)
        net.later(lambda: net.gone(self.along, self.land))

    def block(self, core, k, part):
        start = ((self.spots[k] * 2 + core) * 2 + part) * self.half
        return self.whole.at[pl.ds(pl.multiple_of(start, self.half), self.half)]

    def own(self, k, part):
        return self.landed.at[k % RING, part]

    def pass_over(self, k):
        for part in range(2):
            refs = lambda part=part: (self.block(self.other, k, part), self.own(k, part))
            self.net.send(refs, self.over, self.given[k], "core")

    def passed(self):
        if self.over is not None:
            self.net.gone(self.over, self.landed)
            self.over = None

    def combine(self, k):
        self.net.here(self.given[k], self.landed.at[k % RING])
        for part in range(2):
            here = self.own(k, part)
            here[...] = here[...] + self.block(self.me, k, part)[...]

    def along_x(self, refs, into, by):
        self.net.send(refs, self.along, into, "x", by)

    def start_far(self):
        self.along_x(lambda: (self.own(2, 0), self.land.at[0]), self.through, 1)
        self.along_x(lambda: (self.own(2, 1), self.land.at[1]), self.through, -1)

    def start_right(self):
        self.along_x(lambda: (self.own(1, 1), self.land.at[3]), self.last, 1)

    def start_left(self):
        self.along_x(lambda: (self.own(-1, 0), self.land.at[4]), self.last, -1)

    def forward(self):
        land = self.land
        self.net.here(self.through, land.at[pl.ds(0, 2)])
        land[0] = land[0] + self.own(1, 0)[...]
        self.along_x(lambda: (land.at[0], land.at[2]), self.last, 1)
        land[1] = land[1] + self.own(-1, 1)[...]
        self.along_x(lambda: (land.at[1], land.at[5]), self.last, -1)

    def finish(self, keep):
        land = self.land
        self.net.here(self.last, land.at[pl.ds(2, 4)])
        for part in range(2):
            total = self.own(0, part)[...].astype(F32) + land[2 + part].astype(F32)
            keep(pl.ds(part * self.half, self.half), total + land[4 + part].astype(F32))


ROWS_SCRATCH = (pltpu.VMEM((4, 2, 64, 2048), BF16), pltpu.VMEM((6, 64, 2048), BF16))


class PlaneGather:
    OUT, INTO, LOCALS = 1, 12, 1

    def __init__(self, net, own, whole, spot):
        self.net, self.own, self.whole, self.spot = net, own, whole, spot
        self.rows = own.shape[0]
        self.half = self.rows // 2
        self.width = own.shape[1]
        self.out = net.out()
        self.first = [net.into() for _ in range(2)]
        self.rings = {(color, i): net.into() for color in range(2) for i in (0, 1, -1, -2)}
        self.last = [net.into() for _ in range(2)]
        net.later(lambda: net.gone(self.out, whole.at[pl.ds(0, whole.shape[0] // 16 * 15)]))

    def view(self, color, i, j, part=None):
        place = self.net.place
        first, second = self.axes(color)
        a, b = place.step(first, i), place.step(second, j)
        row, columns = self.spot(a, b) if color == 0 else self.spot(b, a)
        start = row + color * self.half
        if part is None:
            return self.whole.at[pl.ds(pl.multiple_of(start, self.half), self.half), columns]
        size = self.half // 2
        return self.whole.at[pl.ds(pl.multiple_of(start + part * size, size), size), columns]

    def bytes_of(self, halves):
        return self.whole.at[pl.ds(0, halves * self.half), pl.ds(0, self.width)]

    @staticmethod
    def axes(color):
        return ("z", "y") if color == 0 else ("y", "z")

    def mine(self, color):
        return self.own.at[pl.ds(color * self.half, self.half)]

    def ring(self, color, i):
        axis = self.axes(color)[1]
        refs = lambda: (
            self.mine(color) if i == 0 else self.view(color, i, 0), self.view(color, i, 0)
        )
        for by in (1, -1):
            self.net.send(refs, self.out, self.rings[color, i], axis, by)

    def start(self):
        for color in range(2):
            axis = self.axes(color)[0]
            refs = lambda color=color: (self.mine(color), self.view(color, 0, 0))
            for by in (1, -1, 2):
                self.net.send(refs, self.out, self.first[color], axis, by)
        for color in range(2):
            self.ring(color, 0)
        self.kept = self.net.local(self.place_here)

    def place_here(self):
        row, columns = self.spot(self.net.place.z, self.net.place.y)
        return self.own, self.whole.at[pl.ds(pl.multiple_of(row, self.rows), self.rows), columns]

    def spread(self):
        for color in range(2):
            self.net.here(self.first[color], self.bytes_of(3) if self.fits(3) else self.thin(3))
        for i in (-1, 1, -2):
            for color in range(2):
                self.ring(color, i)

    def fits(self, halves):
        return halves * self.half <= self.whole.shape[0]

    def thin(self, halves):
        return self.whole.at[pl.ds(0, self.half), pl.ds(0, halves * self.width)]

    def forward(self, steps=(0, 1, -1, -2)):
        for i in steps:
            for color in range(2):
                axis = self.axes(color)[1]
                self.net.here(self.rings[color, i], self.bytes_of(2))
                for j, part, by in ((-1, 0, 1), (1, 1, -1)):
                    refs = lambda color=color, i=i, j=j, part=part: (
                        self.view(color, i, j, part),
                    ) * 2
                    self.net.send(refs, self.out, self.last[color], axis, by)

    def here(self):
        for color in range(2):
            self.net.here(self.last[color], self.bytes_of(4) if self.fits(4) else self.thin(4))
        self.kept.wait()


class PlaneSum:
    OUT, INTO = 2, 18

    def __init__(self, net, whole, spot, land, last):
        self.net, self.whole, self.spot, self.land, self.last = net, whole, spot, land, last
        self.size = land.shape[3]
        self.ring_out, self.last_out = net.out(), net.out()
        ways = [(color, k) for color in range(2) for k in range(RING)]
        self.through = {way: net.into() for way in ways}
        self.sides = {way: net.into() for way in ways}
        self.ends = [net.into() for _ in range(2)]
        net.later(lambda: net.gone(self.ring_out, land))
        net.later(lambda: net.gone(self.last_out, last))

    @staticmethod
    def axes(color):
        return ("y", "z") if color == 0 else ("z", "y")

    def own(self, color, n, k, part):
        place = self.net.place
        first, second = self.axes(color)
        a, b = place.step(first, n), place.step(second, k)
        row, columns = self.spot(b, a) if color == 0 else self.spot(a, b)
        start = row + (color * 2 + part) * self.size
        return self.whole.at[pl.ds(pl.multiple_of(start, self.size), self.size), columns]

    def slot(self, color, k, n):
        return self.land.at[color, k % RING, n]

    def end(self, color, k, part):
        return self.last.at[color, k % RING - 1, part]

    def start(self):
        for k in (2, 1, -1, 0):
            for color in range(2):
                axis = self.axes(color)[0]
                through, sides = self.through[color, k % RING], self.sides[color, k % RING]
                for n, part, slot, into, by in (
                    (2, 0, 0, through, 1), (2, 1, 1, through, -1),
                    (1, 1, 3, sides, 1), (-1, 0, 4, sides, -1),
                ):
                    refs = lambda color=color, k=k, n=n, part=part, slot=slot: (
                        self.own(color, n, k, part), self.slot(color, k, slot)
                    )
                    self.net.send(refs, self.ring_out, into, axis, by)

    def forward(self, steps=(2, 1, -1, 0)):
        for k in steps:
            for color in range(2):
                axis = self.axes(color)[0]
                sides = self.sides[color, k % RING]
                self.net.here(
                    self.through[color, k % RING], self.land.at[color, k % RING, pl.ds(0, 2)]
                )
                for slot, n, part, target, by in ((0, 1, 0, 2, 1), (1, -1, 1, 5, -1)):
                    here = self.slot(color, k, slot)
                    here[...] = here[...] + self.own(color, n, k, part)[...]
                    refs = lambda color=color, k=k, slot=slot, target=target: (
                        self.slot(color, k, slot), self.slot(color, k, target)
                    )
                    self.net.send(refs, self.ring_out, sides, axis, by)

    def gather(self, steps=(2, 1, -1, 0)):
        for k in steps:
            for color in range(2):
                second = self.axes(color)[1]
                self.net.here(
                    self.sides[color, k % RING], self.land.at[color, k % RING, pl.ds(2, 4)]
                )
                for part in range(2):
                    here = self.slot(color, k, 2 + part)
                    total = self.own(color, 0, k, part)[...].astype(F32) + here[...].astype(F32)
                    total = total + self.slot(color, k, 4 + part)[...].astype(F32)
                    here[...] = total.astype(BF16)
                    if k != 0:
                        refs = lambda color=color, k=k, part=part: (
                            self.slot(color, k, 2 + part), self.end(color, k, part)
                        )
                        self.net.send(refs, self.last_out, self.ends[color], second, k)

    def finish(self, total):
        for color in range(2):
            self.net.here(self.ends[color], self.last.at[color])
            for part in range(2):
                value = self.slot(color, 0, 2 + part)[...].astype(F32)
                for k in (1, -1, 2):
                    value = value + self.end(color, k, part)[...].astype(F32)
                start = (color * 2 + part) * self.size
                total[pl.ds(start, self.size)] = value.astype(total.dtype)


def plane_scratch(rows, columns):
    return (
        pltpu.VMEM((2, 4, 6, rows // 4, columns), BF16),
        pltpu.VMEM((2, 3, 2, rows // 4, columns), BF16),
    )


class Turn:
    def __init__(self, net, pairs):
        self.net = net
        self.pairs = [
            (source, target, net.out(), net.into(), net.local_number()) for source, target in pairs
        ]

    def copies(self):
        return [self.net.copy(a, b, out, into, "turn") for a, b, out, into, _ in self.pairs]

    def kept(self):
        sems = self.net.local_sems
        return [pltpu.make_async_copy(a, b, sems.at[index]) for a, b, _, _, index in self.pairs]

    def both(self, act):
        @pl.when(jnp.logical_not(self.net.place.native))
        def _():
            for copy in self.copies():
                act(copy)

        @pl.when(self.net.place.native)
        def _():
            for copy in self.kept():
                act(copy)

    def start(self):
        self.both(lambda copy: copy.start())

    def wait(self):
        self.both(lambda copy: copy.wait())


class Give:
    def __init__(self, net, refs, there):
        self.net, self.there = net, there
        self.out, self.into = net.out(), net.into()
        net.send(refs, self.out, self.into, "core")
        net.later(lambda: net.gone(self.out, refs()[0]))

    def wait(self):
        self.net.here(self.into, self.there())


def parts_of(source, target, count):
    rows = source.shape[0] // count
    spots = [pl.ds(part * rows, rows) for part in range(count)]
    return [(source.at[spot], target.at[spot]) for spot in spots]


class GainsGather:
    OUT, INTO, LOCALS = 1, 4, 1

    def __init__(self, net, own, whole):
        self.net, self.own, self.whole = net, own, whole
        self.out = net.out()
        self.into = [net.into() for _ in range(4)]
        net.later(lambda: net.gone(self.out, whole.at[pl.ds(0, 127)]))

    def rows(self, z, y, x, core, count):
        start = ((z * RING + y) * RING + x) * 2 + core
        return self.whole.at[pl.ds(start if count == 1 else pl.multiple_of(start, count), count)]

    def spot(self, axis, by):
        place = self.net.place
        if axis == "core":
            return self.rows(place.z, place.y, place.x, (place.core + by) % 2, 1)
        if axis == "x":
            return self.rows(place.z, place.y, place.step("x", by), 0, 2)
        if axis == "y":
            return self.rows(place.z, place.step("y", by), 0, 0, 8)
        return self.rows(place.step("z", by), 0, 0, 0, 32)

    def steps(self):
        net = self.net
        net.local(lambda: (self.own, self.spot("core", 0))).wait()
        for into, axis, count in zip(self.into, ("core", "x", "y", "z"), (1, 2, 8, 32)):
            ways = (1,) if axis == "core" else (1, -1, 2)
            for by in ways:
                net.send(lambda: (self.spot(axis, 0),) * 2, self.out, into, axis, by)
            yield
            net.here(into, self.whole.at[pl.ds(0, count * len(ways))])
        yield


class GainsSum(GainsGather):
    def __init__(self, net, whole, total, land):
        super().__init__(net, None, whole)
        self.total, self.land = total, land

    def steps(self):
        net, land = self.net, self.land
        first = 0
        for into, axis, count in zip(self.into, ("z", "y", "x", "core"), (32, 8, 2, 1)):
            ways = (1,) if axis == "core" else (1, -1, 2)
            spots = [pl.ds(first + n * count, count) for n in range(len(ways))]
            for spot, by in zip(spots, ways):
                refs = lambda spot=spot, by=by: (self.spot(axis, by), land.at[spot])
                net.send(refs, self.out, into, axis, by)
            yield
            net.here(into, land.at[pl.ds(first, count * len(ways))])
            value = self.spot(axis, 0)[...]
            for spot in spots:
                value = value + land[spot]
            if axis == "core":
                self.total[...] = value
            else:
                self.spot(axis, 0)[...] = value
            first += count * len(ways)
        yield


class Kernel:
    def __init__(self, number, plans, gives, turns, locals_, partners):
        self.number, self.partners = number, partners
        extra = gives + turns
        self.sems = (
            sum(plan.OUT for plan in plans) + extra,
            sum(plan.INTO for plan in plans) + extra,
            sum(getattr(plan, "LOCALS", 0) for plan in plans) + turns + locals_,
        )

    def __call__(self, body, arrays, outs, scratch=()):
        n_in, n_out, n_scratch = len(arrays), len(outs), len(scratch)

        def kernel(*refs):
            net = Net(Place(), self.partners, *refs[n_in + n_out + n_scratch :])
            net.greet()
            body(
                net,
                refs[:n_in],
                refs[n_in : n_in + n_out],
                refs[n_in + n_out : n_in + n_out + n_scratch],
            )
            net.finish()
            assert (net.leaving, net.arriving, net.local_count) == self.sems, (
                net.leaving, net.arriving, net.local_count, self.sems,
            )

        return pl.pallas_call(
            kernel,
            out_shape=[shape for shape, _ in outs],
            in_specs=[pl.BlockSpec(memory_space=space) for _, space in arrays],
            out_specs=[pl.BlockSpec(memory_space=space) for _, space in outs],
            scratch_shapes=[*scratch] + [pltpu.SemaphoreType.DMA((n,)) for n in self.sems],
            compiler_params=pltpu.CompilerParams(
                collective_id=self.number, has_side_effects=True, vmem_limit_bytes=61 * 2**20
            ),
            name="links_%d" % self.number,
        )(*[array for array, _ in arrays])


CORE_PARTNER = (("core", 1),)
X_PARTNERS = (("x", 1), ("x", -1))
FAR_X = (("x", 2),)
PLANE_PARTNERS = (("y", 1), ("y", -1), ("y", 2), ("z", 1), ("z", -1), ("z", 2))
TURN_PARTNERS = (("turn", 1),)


def shape(dims, dtype=BF16):
    return jax.ShapeDtypeStruct(dims, dtype)


def attention_spot(z, y):
    piece = z * 4 + lax.rem(y, 2) * 2 + lax.div(y, 2)
    return piece * 128


def rows_spot(z, y):
    return attention_spot(z, y), pl.ds(0, 512)


def output_spot(z, y):
    return 0, pl.ds(pl.multiple_of(attention_spot(z, y), 128), 128)


def gateup_spot(z, y):
    columns = pl.ds(pl.multiple_of(lax.div(y, 2) * 384, 128), 384)
    return (z * 2 + lax.rem(y, 2)) * 256, columns


def down_spot(z, y):
    columns = pl.ds(pl.multiple_of((z * 2 + lax.rem(y, 2)) * 256, 128), 256)
    return lax.div(y, 2) * 384, columns


def nn(left, right):
    return lax.dot_general(left, right, (((1,), (0,)), ((), ())), preferred_element_type=F32)


def nt(left, right):
    return lax.dot_general(left, right, (((1,), (1,)), ((), ())), preferred_element_type=F32)


def tn(left, right):
    return lax.dot_general(left, right, (((0,), (0,)), ((), ())), preferred_element_type=F32)


def exact(left, right):
    return lax.dot_general(
        left, right, (((1,), (0,)), ((), ())),
        precision=lax.Precision.HIGHEST, preferred_element_type=F32,
    )


def inverse_root(rows):
    return lax.rsqrt(jnp.mean(rows * rows, axis=-1, keepdims=True) + EPSILON)


def norm_back(rows, gain, upstream):
    root = inverse_root(rows)
    weighted = upstream * gain
    meant = jnp.mean(weighted * rows, axis=-1, keepdims=True)
    return root * weighted - rows * (root * root * root * meant), upstream * rows * root


def rope_tables():
    halves = np.arange(HEAD_SIZE // 2, dtype=np.float64)
    angles = np.arange(GROUP_TOK)[:, None] * ROPE_BASE ** (-2.0 * halves / HEAD_SIZE)[None, :]
    angles = np.concatenate([angles, angles], axis=1)
    return np.cos(angles).astype(np.float32), np.sin(angles).astype(np.float32)


def owner_starts(dims, axis):
    row = lax.broadcasted_iota(jnp.int32, dims, axis)
    z, y, x, core = row >> 5, (row >> 3) & 3, (row >> 1) & 3, row & 1
    return (z * 32 + (y & 1) * 16 + core * 8 + (y >> 1) * 4 + x) * OWN_GAINS


def column_of(entry):
    return entry - jnp.floor((entry.astype(F32) + 0.5) * (1.0 / OWN_GAINS)).astype(jnp.int32) * OWN_GAINS


def gains_flat(rows):
    entry = lax.broadcasted_iota(jnp.int32, (128, GAINS), 1)
    past = entry - owner_starts((128, GAINS), 0)
    owner = ((past >= 0) & (past < OWN_GAINS)).astype(F32)
    columns = lax.dot_general(
        rows, owner, (((0,), (0,)), ((), ())),
        precision=lax.Precision.HIGHEST, preferred_element_type=F32,
    )
    place = lax.broadcasted_iota(jnp.int32, (128, GAINS), 0)
    return jnp.sum(jnp.where(column_of(entry) == place, columns, 0.0), axis=0, keepdims=True)


class Documents:
    def __init__(self, lengths):
        lengths = [lengths[0:1, n : n + 1] for n in range(4)]
        self.ends = [lengths[0], lengths[0] + lengths[1], lengths[0] + lengths[1] + lengths[2]]

    def pick(self, place, values):
        value = jnp.where(place >= self.ends[0], values[1], values[0])
        value = jnp.where(place >= self.ends[1], values[2], value)
        return jnp.where(place >= self.ends[2], values[3], value)

    def first(self, place):
        zero = jnp.zeros_like(self.ends[0])
        return self.pick(place, [zero] + self.ends)


def allowed_pairs(documents, first_row, rows, keys):
    query = lax.broadcasted_iota(jnp.int32, (rows, 1), 0) + first_row
    key = lax.broadcasted_iota(jnp.int32, (rows, keys), 1)
    return (key >= documents.first(query)) & (key <= query)


def unit_off(n):
    return lax.rem(n + lax.div(n, 2), 4) + 2 * lax.div(n, 3)


class Units:
    ORDER = (0, 1, -1, 2)

    def __init__(self, place):
        self.x = place.x

    def chip(self, n):
        return lax.rem(self.x + unit_off(n), RING)

    def rows(self, n):
        return pl.ds(pl.multiple_of(self.chip(n) * 256, 256), 256)

    def true_rows(self, n, core):
        return pl.ds(pl.multiple_of((core * RING + self.chip(n)) * 128, 128), 128)


def own_half(length, core):
    return pl.ds(pl.multiple_of(core * length, 128), length)


def attention_forward(
    tokens, cotangent, query, keyval, output, gateup, down, gains, lengths, cosine, sine
):
    def body(net, ins, outs, work):
        (
            tokens_, cotangent_, query_, keyval_, output_, gateup_, down_, gains_, lengths_,
            cosine_, sine_,
        ) = ins
        (
            residual_, tokens_here, cotangent_here, normed_, raw_, heads_, attended_, totals_,
            cosine_out, sine_out, qkv_out, output_out, gate_out, up_out, down_piece,
            cotangent_all, flat_, lengths_out,
        ) = outs
        (
            gathered, normed, qkv_w, output_w, qkv_cast, output_cast, qkv_piece, output_piece,
            gains_row, gains_rows, lengths_mine, lengths_there, gate_cast, up_cast, down_cast,
            gate_piece, up_piece, terms, landed, land,
        ) = work
        place = net.place
        units = Units(place)
        mine, theirs = place.core, 1 - place.core

        qkv_cast[:, 0:256] = query_[...].astype(BF16)
        qkv_cast[:, 256:384] = keyval_[0].astype(BF16)
        qkv_cast[:, 384:512] = keyval_[1].astype(BF16)
        output_cast[...] = output_[...].astype(BF16)
        gains_row[0] = jnp.zeros((1, 128), F32)
        gains_row[0, 0:1, 0:OWN_GAINS] = gains_[...]
        lengths_mine[...] = jnp.zeros((8, 128), jnp.int32)
        lengths_mine[0:1, 0:4] = lengths_[...]
        net.enter()
        qkv_turn = Turn(net, [(qkv_cast, qkv_piece)])
        output_turn = Turn(net, [(output_cast, output_piece)])
        rows = [Turn(net, [pair]) for pair in parts_of(tokens_, tokens_here, 2)]
        upstream = Turn(net, parts_of(cotangent_, cotangent_here, 2))
        qkv_turn.start()
        for part in rows:
            part.start()
        qkv_gather = PlaneGather(net, qkv_piece, qkv_w, rows_spot)
        output_gather = PlaneGather(net, output_piece, output_w, output_spot)
        gate_gather = PlaneGather(net, gate_piece, gate_out, gateup_spot)
        up_gather = PlaneGather(net, up_piece, up_out, gateup_spot)
        gather = RowsGather(net, tokens_here, gathered)
        later = RowsGather(net, cotangent_here, cotangent_all)
        length_copy = Give(net, lambda: (lengths_mine, lengths_there), lambda: lengths_there)
        gains_steps = GainsGather(net, gains_row, gains_rows).steps()
        next(gains_steps)

        halves = []
        for n, (cast, piece) in enumerate(((gate_cast, gate_piece), (up_cast, up_piece))):
            spot = own_half(128, mine)
            piece[spot] = gateup_[n, :, own_half(384, mine)].astype(BF16)
            cast[...] = gateup_[n, :, own_half(384, theirs)].astype(BF16)
            halves.append(Give(
                net,
                lambda cast=cast, piece=piece: (cast, piece.at[own_half(128, mine)]),
                lambda piece=piece: piece.at[own_half(128, theirs)],
            ))
        down_piece[:, own_half(128, mine)] = down_[own_half(384, mine)].astype(BF16)
        down_cast[...] = down_[own_half(384, theirs)].astype(BF16)
        halves.append(Give(
            net,
            lambda: (down_cast, down_piece.at[:, own_half(128, mine)]),
            lambda: down_piece.at[:, own_half(128, theirs)],
        ))

        qkv_turn.wait()
        qkv_gather.start()
        output_turn.start()
        for n, part in enumerate(rows):
            part.wait()
            gather.start((n,))
        upstream.start()
        next(gains_steps)

        length_copy.wait()
        lengths_out[...] = jnp.where(place.native, lengths_mine[...], lengths_there[...])
        documents = Documents(lengths_out[...])
        zero = jnp.zeros((1, 1), jnp.int32)
        starts = [zero] + documents.ends
        everywhere = lax.broadcasted_iota(jnp.int32, (1, GROUP_TOK), 1)
        hits = jnp.concatenate(
            [(everywhere == start).astype(F32) for start in starts] * 2, axis=0
        )
        start_cosine = exact(hits, cosine_[...])
        start_sine = exact(hits, sine_[...])
        sign = jnp.where(lax.broadcasted_iota(jnp.int32, (1, HEAD_SIZE), 1) < 64, -1.0, 1.0)

        def table(n):
            spot = pl.ds(pl.multiple_of(n * 256, 256), 256)
            where = lax.broadcasted_iota(jnp.int32, (256, 1), 0) + n * 256
            cosine_by = documents.pick(where, [start_cosine[n : n + 1] for n in range(4)])
            sine_by = documents.pick(where, [start_sine[n : n + 1] for n in range(4)])
            cosine_out[spot] = cosine_[spot] * cosine_by + sine_[spot] * sine_by
            sine_out[spot] = (sine_[spot] * cosine_by - cosine_[spot] * sine_by) * sign

        staged(4, table)
        qkv_gather.spread()
        output_turn.wait()
        output_gather.start()
        next(gains_steps)
        gather.near_first()
        for half in halves:
            half.wait()
        next(gains_steps)
        qkv_gather.forward()
        output_gather.spread()
        gate_gather.start()
        next(gains_steps)
        flat_[...] = gains_flat(gains_rows[...].reshape(128, 128))
        gain_query = flat_[0:1, 4096:4224]
        gain_key = flat_[0:1, 4224:4352]

        def normalize(n):
            rows_in = gathered[units.rows(n)].astype(F32)
            normed[units.rows(n)] = (
                rows_in * inverse_root(rows_in) * flat_[0:1, 0:2048]
            ).astype(BF16)

        def near():
            gather.near_second()
            gather.here(1)

        def far():
            gather.far()
            output_gather.forward()
            up_gather.start()
            upstream.wait()
            later.start()
            gather.here(2)

        staged(4, normalize, {
            0: lambda: gather.here(0), 1: near, 2: lambda: gather.here(-1), 3: far,
        })
        qkv_gather.here()
        stores = [net.local(lambda: (normed, normed_)), net.local(lambda: (qkv_w, qkv_out))]

        def project(n):
            parts = nn(normed[units.rows(n)], qkv_w[...])
            for core in range(2):
                spot = units.true_rows(n, core)
                part = parts[core * 128 : core * 128 + 128]
                raw_[spot] = part[:, 0:384]
                heads_[spot, 384:512] = part[:, 384:512].astype(BF16)
                for head in range(3):
                    columns = slice(head * 128, head * 128 + 128)
                    value = part[:, columns]
                    value = value * inverse_root(value) * (gain_key if head == 2 else gain_query)
                    turned = value * cosine_out[spot] + pltpu.roll(value, 64, 1) * sine_out[spot]
                    heads_[spot, columns] = turned.astype(BF16)

        staged(4, project)
        gate_gather.spread()

        def attend(block):
            keys = 256 * (block + 1)
            spot = slice(block * 256, block * 256 + 256)

            def one(head):
                columns = own_half(128, head)
                scores = nt(heads_[spot, columns], heads_[0:keys, 256:384])
                allowed = allowed_pairs(documents, block * 256, 256, keys)
                scores = jnp.where(allowed, scores, -1e30)
                highest = jnp.max(scores, axis=-1, keepdims=True)
                weights_ = jnp.exp((scores - highest) * SCALE)
                summed = jnp.sum(weights_, axis=-1, keepdims=True)
                probability = (weights_ * (1.0 / summed)).astype(BF16)
                attended_[spot, columns] = nn(probability, heads_[0:keys, 384:512]).astype(BF16)
                totals_[spot, columns] = jnp.broadcast_to(
                    highest * SCALE + jnp.log(summed), (256, 128)
                )

            staged(2, one)

        attend(0)
        attend(1)
        later.near_first()
        up_gather.spread()
        attend(2)
        output_gather.here()
        stores.append(net.local(lambda: (output_w, output_out)))
        attend(3)
        sums = RowsSum(net, terms, landed, land)

        def out(n):
            n = 3 - n
            own = jnp.concatenate(
                [attended_[units.true_rows(n, 0)], attended_[units.true_rows(n, 1)]], axis=0
            )
            terms[units.rows(n)] = nn(own, output_w[...]).astype(BF16)

        def passed(k, ready=None, go=None):
            def act():
                sums.pass_over(k)
                if ready is not None:
                    sums.combine(ready)
                    go()

            return act

        later.near_second()
        staged(4, out, None, {
            0: passed(2),
            1: passed(-1, 2, sums.start_far),
            2: passed(1, -1, sums.start_left),
            3: passed(0, 1, sums.start_right),
        })
        later.far()
        gate_gather.forward()
        sums.combine(0)
        sums.forward()
        up_gather.forward()
        for k in (0, 1, -1, 2):
            later.here(k)

        def keep(spot, value):
            residual_[spot] = value + tokens_here[spot].astype(F32)

        sums.finish(keep)
        gate_gather.here()
        up_gather.here()
        for store in stores:
            store.wait()

    plans = (GainsGather,) + 4 * (PlaneGather,) + 2 * (RowsGather,) + (RowsSum,)
    return Kernel(
        0, plans, 4, 6, 3, CORE_PARTNER + X_PARTNERS + FAR_X + PLANE_PARTNERS + TURN_PARTNERS
    )(
        body,
        [
            (tokens, VMEM), (cotangent, VMEM), (query, VMEM), (keyval, VMEM), (output, VMEM),
            (gateup, VMEM), (down, VMEM), (gains, VMEM), (lengths, VMEM),
            (cosine, VMEM), (sine, VMEM),
        ],
        [
            (shape((128, 2048), F32), VMEM),
            (shape((128, 2048)), VMEM),
            (shape((128, 2048)), VMEM),
            (shape((1024, 2048)), HBM),
            (shape((1024, 384), F32), VMEM),
            (shape((1024, 512)), VMEM),
            (shape((1024, 256)), VMEM),
            (shape((1024, 256), F32), VMEM),
            (shape((1024, 128), F32), VMEM),
            (shape((1024, 128), F32), VMEM),
            (shape((2048, 512)), HBM),
            (shape((256, 2048)), HBM),
            (shape((2048, 768)), HBM),
            (shape((2048, 768)), HBM),
            (shape((384, 256)), VMEM),
            (shape((1024, 2048)), HBM),
            (shape((1, GAINS), F32), VMEM),
            (shape((8, 128), jnp.int32), VMEM),
        ],
        (
            pltpu.VMEM((1024, 2048), BF16),
            pltpu.VMEM((1024, 2048), BF16),
            pltpu.VMEM((2048, 512), BF16),
            pltpu.VMEM((256, 2048), BF16),
            pltpu.VMEM((128, 512), BF16),
            pltpu.VMEM((256, 128), BF16),
            pltpu.VMEM((128, 512), BF16),
            pltpu.VMEM((256, 128), BF16),
            pltpu.VMEM((1, 1, 128), F32),
            pltpu.VMEM((128, 1, 128), F32),
            pltpu.VMEM((8, 128), jnp.int32),
            pltpu.VMEM((8, 128), jnp.int32),
            pltpu.VMEM((128, 384), BF16),
            pltpu.VMEM((128, 384), BF16),
            pltpu.VMEM((384, 128), BF16),
            pltpu.VMEM((256, 384), BF16),
            pltpu.VMEM((256, 384), BF16),
            pltpu.VMEM((1024, 2048), BF16),
        )
        + ROWS_SCRATCH,
    )


def feed_forward(residual, cotangent, gains, cotangent_all, gate, up, down):
    def body(net, ins, outs, work):
        residual_, cotangent_, gains_, cotangent_all_, gate_, up_, down_ = ins
        back_, low_, gain_grad_, mlp_, gate_grad_, up_grad_, down_grad_ = outs
        (
            second_low, second, upstream, gate_w, up_w, down_w, hidden, gate_low, up_low, terms,
            mlp, gate_g, up_g, down_g, landed, land,
        ) = work
        place = net.place
        units = Units(place)
        gain = gains_[0:1, 2048:4096]
        rows = residual_[...]
        second_low[...] = (rows * inverse_root(rows) * gain).astype(BF16)
        loads = [
            net.local(lambda: (gate_, gate_w)),
            net.local(lambda: (up_, up_w)),
            net.local(lambda: (cotangent_all_, upstream)),
        ]
        net.enter()
        gather = RowsGather(net, second_low, second)
        gather.start()
        down_gather = PlaneGather(net, down_, down_w, down_spot)
        down_gather.start()
        sums = RowsSum(net, terms, landed, land)

        def forth(n):
            spot = units.rows(n)
            gate_value = nn(second[spot], gate_w[...])
            upward = nn(second[spot], up_w[...])
            sigmoid = 1.0 / (1.0 + jnp.exp(-gate_value))
            active = gate_value * sigmoid
            hidden[spot] = (active * upward).astype(BF16)
            gate_low[spot] = (upward * (sigmoid + active * (1.0 - sigmoid))).astype(BF16)
            up_low[spot] = active.astype(BF16)

        def begin():
            loads[0].wait()
            loads[1].wait()
            gather.here(0)

        def near():
            gather.near_first()
            down_gather.spread()
            gather.near_second()
            gather.here(1)

        def far():
            down_gather.forward()
            gather.far()
            gather.here(2)

        staged(4, forth, {0: begin, 1: near, 2: lambda: gather.here(-1), 3: far})
        down_gather.here()

        def back(n):
            spot = units.rows(3 - n)
            hidden_grad = nt(upstream[spot], down_w[...])
            gate_low[spot] = (hidden_grad * gate_low[spot].astype(F32)).astype(BF16)
            up_low[spot] = (hidden_grad * up_low[spot].astype(F32)).astype(BF16)
            terms[spot] = (nt(gate_low[spot], gate_w[...]) + nt(up_low[spot], up_w[...])).astype(
                BF16
            )

        def passed(k, ready=None, go=None):
            def act():
                sums.pass_over(k)
                if ready is not None:
                    sums.combine(ready)
                    go()

            return act

        loads[2].wait()
        staged(4, back, None, {
            0: passed(2),
            1: passed(-1, 2, sums.start_far),
            2: passed(1, -1, sums.start_left),
            3: passed(0, 1, sums.start_right),
        })
        def down_grad(n):
            columns = own_half(256, n)
            down_g[columns] = tn(hidden[:, columns], upstream[...]).astype(BF16)

        staged(3, down_grad, None, {2: lambda: (sums.combine(0), sums.forward())})
        stores = [net.local(lambda: (down_g, down_grad_))]

        def weight_grad(low, target):
            def one(n):
                columns = own_half(256, n)
                target[columns] = tn(second[:, columns], low[...]).astype(BF16)

            return one

        staged(8, weight_grad(gate_low, gate_g))
        stores.append(net.local(lambda: (gate_g, gate_grad_)))
        gain_parts = []

        def keep(spot, value):
            through, gain_part = norm_back(residual_[spot], gain, value)
            through = through + cotangent_[spot].astype(F32)
            back_[spot] = through
            low_[spot] = through.astype(BF16)
            gain_parts.append(jnp.sum(gain_part, axis=0, keepdims=True))

        def through(n):
            spot = units.rows(n)
            mlp[spot] = nn(hidden[spot], down_w[...]).astype(BF16)

        staged(4, through)
        stores.append(net.local(lambda: (mlp, mlp_)))
        staged(8, weight_grad(up_low, up_g))
        stores.append(net.local(lambda: (up_g, up_grad_)))
        sums.finish(keep)
        gain_grad_[...] = gain_parts[0] + gain_parts[1]
        for store in stores:
            store.wait()

    plans = (RowsGather, RowsSum, PlaneGather)
    return Kernel(1, plans, 0, 0, 3 + 4, CORE_PARTNER + X_PARTNERS + PLANE_PARTNERS)(
        body,
        [
            (residual, VMEM), (cotangent, VMEM), (gains, VMEM),
            (cotangent_all, HBM), (gate, HBM), (up, HBM), (down, VMEM),
        ],
        [
            (shape((128, 2048), F32), VMEM),
            (shape((128, 2048)), VMEM),
            (shape((1, 2048), F32), VMEM),
            (shape((1024, 2048)), HBM),
            (shape((2048, 768)), HBM),
            (shape((2048, 768)), HBM),
            (shape((768, 2048)), HBM),
        ],
        (
            pltpu.VMEM((128, 2048), BF16),
            pltpu.VMEM((1024, 2048), BF16),
            pltpu.VMEM((1024, 2048), BF16),
            pltpu.VMEM((2048, 768), BF16),
            pltpu.VMEM((2048, 768), BF16),
            pltpu.VMEM((768, 2048), BF16),
            pltpu.VMEM((1024, 768), BF16),
            pltpu.VMEM((1024, 768), BF16),
            pltpu.VMEM((1024, 768), BF16),
            pltpu.VMEM((1024, 2048), BF16),
            pltpu.VMEM((1024, 2048), BF16),
            pltpu.VMEM((2048, 768), BF16),
            pltpu.VMEM((2048, 768), BF16),
            pltpu.VMEM((768, 2048), BF16),
        )
        + ROWS_SCRATCH,
    )


def attention_backward(
    low, back, residual, tokens, gains, second_gain, heads, raw, attended, totals, cosine, sine,
    lengths, qkv, output, normed, mlp, gate, up, down,
):
    def body(net, ins, outs, work):
        (
            low_, back_, residual_, tokens_, gains_, second_gain_, heads_, raw_, attended_, totals_,
            cosine_, sine_, lengths_, qkv_, output_, normed_, mlp_, gate_, up_, down_,
        ) = ins
        (
            block_own, input_own, qkv_own, output_own, gate_own, up_own, down_own, gains_own,
        ) = outs
        (
            rows, terms, qkv_w, output_w, gate_g, up_g, down_g, qkv_g, output_g,
            attended_rows, attended_grad, key_sum, value_sum, parts,
            block_out, input_out, qkv_total, output_total, gate_total, up_total, down_total,
            gain_rows, gain_land,
            mlp_landed, mlp_land, first_landed, first_land,
            gate_land, gate_last, up_land, up_last, down_land, down_last,
            qkv_land, qkv_last, output_land, output_last,
        ) = work
        place = net.place
        units = Units(place)
        mine, theirs = place.core, 1 - place.core
        loads = {
            name: net.local(lambda source=source, target=target: (source, target))
            for name, source, target in (
                ("gate", gate_, gate_g), ("up", up_, up_g), ("output", output_, output_w),
                ("down", down_, down_g), ("mlp", mlp_, terms), ("qkv", qkv_, qkv_w),
            )
        }
        gather = RowsGather(net, low_, rows)
        gate_sum = PlaneSum(net, gate_g, gateup_spot, gate_land, gate_last)
        up_sum = PlaneSum(net, up_g, gateup_spot, up_land, up_last)
        down_sum = PlaneSum(net, down_g, down_spot, down_land, down_last)
        qkv_sum = PlaneSum(net, qkv_g, rows_spot, qkv_land, qkv_last)
        output_sum = PlaneSum(net, output_g, output_spot, output_land, output_last)
        mlp_sum = RowsSum(net, terms, mlp_landed, mlp_land)
        first_sum = RowsSum(net, terms, first_landed, first_land)

        def same_order(n):
            for core in range(2):
                start = pl.multiple_of(units.chip(n) * 256 + core * 128, 128)
                attended_rows[pl.ds(start, 128)] = attended_[units.true_rows(n, core)]

        staged(4, same_order)
        key_sum[...] = jnp.zeros_like(key_sum)
        value_sum[...] = jnp.zeros_like(value_sum)
        net.enter()
        gather.start()
        loads["gate"].wait()
        gate_sum.start()
        loads["up"].wait()
        up_sum.start()
        loads["output"].wait()

        halves = []

        def exchange(cut, there):
            halves.append(net.local(lambda: (cut(mine), there(mine))))
            halves.append(
                Give(net, lambda: (cut(theirs), there(mine)), lambda: there(theirs))
            )

        def enter(n):
            grad = nt(rows[units.rows(n)], output_w[...]).astype(BF16)
            for core in range(2):
                attended_grad[units.true_rows(n, core)] = grad[core * 128 : core * 128 + 128]

        def near():
            loads["down"].wait()
            down_sum.start()
            loads["mlp"].wait()
            for k in (2, 1, -1, 0):
                mlp_sum.pass_over(k)
            gather.near_first()
            gather.near_second()
            for k in (2, 1, -1, 0):
                mlp_sum.combine(k)
            gather.here(1)

        def far():
            gather.far()
            mlp_sum.start_far()
            mlp_sum.start_right()
            mlp_sum.start_left()
            gather.here(2)

        staged(4, enter, {0: lambda: gather.here(0), 1: near, 2: lambda: gather.here(-1), 3: far})

        def output_grad(n):
            columns = own_half(512, n)
            output_g[:, columns] = tn(attended_rows[...], rows[:, columns]).astype(BF16)

        staged(4, output_grad)
        output_sum.start()
        gate_sum.forward()
        gather.gone()
        loads["normed"] = net.local(lambda: (normed_, rows))

        documents = Documents(lengths_[...])
        gain_query, gain_key = gains_[0:1, 4096:4224], gains_[0:1, 4224:4352]

        def through_rope(value, spot, raw_part, gain):
            value = value * cosine_[spot] + pltpu.roll(value * sine_[spot], 64, 1)
            through, gain_part = norm_back(raw_part, gain, value)
            return through.astype(BF16), jnp.sum(gain_part, axis=0, keepdims=True)

        def attend(block, gain_sum):
            keys = 256 * (block + 1)
            spot = slice(block * 256, block * 256 + 256)

            def one(head, gain_sum):
                columns = own_half(128, head)
                query, upstream = heads_[spot, columns], attended_grad[spot, columns]
                key, value = heads_[0:keys, 256:384], heads_[0:keys, 384:512]
                scores = nt(query, key) * SCALE
                total = totals_[spot, columns][:, 0:1]
                allowed = allowed_pairs(documents, block * 256, 256, keys)
                probability = jnp.where(allowed, jnp.exp(scores - total), 0.0)
                prob_grad = nt(upstream, value)
                centre = jnp.sum(probability * prob_grad, axis=-1, keepdims=True)
                score_grad = (probability * (prob_grad - centre)).astype(BF16)
                value_sum[0:keys] += tn(probability.astype(BF16), upstream)
                key_sum[0:keys] += tn(score_grad, query)
                query_grad = nn(score_grad, key) * SCALE
                through, gain_part = through_rope(query_grad, spot, raw_[spot, columns], gain_query)
                for n in range(2):
                    true = block * 2 + n
                    start = ((true % RING) * 2 + true // RING) * 128
                    parts[start : start + 128, columns] = through[n * 128 : n * 128 + 128]
                return gain_sum + gain_part

            return lax.fori_loop(0, 2, one, gain_sum)

        query_gain = attend(3, jnp.zeros((1, 128), F32))
        up_sum.forward()
        mlp_sum.forward()
        query_gain = attend(2, query_gain)
        down_sum.forward()
        query_gain = attend(1, query_gain)
        query_gain = attend(0, query_gain)
        gate_sum.gather()

        def keep_block(spot, value):
            block_out[spot] = (residual_[spot] + value).astype(BF16)

        def key_back(true, gain_sum):
            spot = pl.ds(pl.multiple_of(true * 128, 128), 128)
            start = (lax.rem(true, RING) * 2 + lax.div(true, RING)) * 128
            through, gain_part = through_rope(
                key_sum[spot] * SCALE, spot, raw_[spot, 256:384], gain_key
            )
            here = pl.ds(pl.multiple_of(start, 128), 128)
            parts[here, 256:384] = through
            parts[here, 384:512] = value_sum[spot].astype(BF16)
            return gain_sum + gain_part

        key_gain = lax.fori_loop(0, 8, key_back, jnp.zeros((1, 128), F32))
        mlp_sum.passed()
        loads["qkv"].wait()

        def out(n):
            spot = units.rows(3 - n)
            terms[spot] = nt(parts[spot], qkv_w[...]).astype(BF16)

        def passed(k, ready=None, go=None):
            def act():
                first_sum.pass_over(k)
                if ready is not None:
                    first_sum.combine(ready)
                    go()

            return act

        staged(4, out, None, {
            0: passed(2),
            1: passed(-1, 2, first_sum.start_far),
            2: passed(1, -1, first_sum.start_left),
            3: passed(0, 1, first_sum.start_right),
        })
        loads["normed"].wait()

        def qkv_grad(n):
            columns = own_half(256, n)
            qkv_g[columns] = tn(rows[:, columns], parts[...]).astype(BF16)

        staged(8, qkv_grad, None, {3: lambda: (first_sum.combine(0), first_sum.forward())})
        qkv_sum.start()
        up_sum.gather()
        output_sum.forward()
        down_sum.gather()
        mlp_sum.finish(keep_block)
        block_turn = Turn(net, parts_of(block_out, block_own, 2))
        block_turn.start()
        gate_sum.finish(gate_total)
        output_sum.gather()
        qkv_sum.forward()
        up_sum.finish(up_total)
        for source, target in ((gate_total, gate_own), (up_total, up_own)):
            exchange(
                lambda core, source=source: source.at[own_half(128, core)],
                lambda core, target=target: target.at[:, own_half(384, core)],
            )

        gain_parts = []
        turns = []

        def keep_first(spot, value):
            rows_in = tokens_[spot].astype(F32)
            through, gain_part = norm_back(rows_in, gains_[0:1, 0:2048], value)
            input_out[spot] = (back_[spot] + through).astype(BF16)
            gain_parts.append(jnp.sum(gain_part, axis=0, keepdims=True))
            turns.append(Turn(net, [(input_out.at[spot], input_own.at[spot])]))
            turns[-1].start()

        first_sum.finish(keep_first)
        flat = jnp.concatenate(
            [gain_parts[0] + gain_parts[1], second_gain_[...], query_gain, key_gain], axis=1
        )
        entry = lax.broadcasted_iota(jnp.int32, (128, GAINS), 1)
        past = entry - owner_starts((128, GAINS), 0)
        owned = jnp.where((past >= 0) & (past < OWN_GAINS), flat, 0.0)
        column = (column_of(entry) == lax.broadcasted_iota(jnp.int32, (128, GAINS), 0)).astype(F32)
        gain_rows[...] = lax.dot_general(
            owned, column, (((1,), (1,)), ((), ())),
            precision=lax.Precision.HIGHEST, preferred_element_type=F32,
        ).reshape(128, 1, 128)
        gains_steps = GainsSum(net, gain_rows, gains_own, gain_land).steps()
        next(gains_steps)
        down_sum.finish(down_total)
        exchange(
            lambda core: down_total.at[:, own_half(128, core)],
            lambda core: down_own.at[own_half(384, core)],
        )
        output_sum.finish(output_total)
        output_turn = Turn(net, [(output_total, output_own)])
        output_turn.start()
        next(gains_steps)
        qkv_sum.gather()
        next(gains_steps)
        next(gains_steps)
        qkv_sum.finish(qkv_total)
        qkv_turn = Turn(net, [(qkv_total, qkv_own)])
        qkv_turn.start()
        next(gains_steps)
        for copy in halves:
            copy.wait()
        for turn in (block_turn, output_turn, *turns, qkv_turn):
            turn.wait()

    plans = (RowsGather,) + 2 * (RowsSum,) + 5 * (PlaneSum,) + (GainsSum,)
    return Kernel(
        2, plans, 3, 6, 7 + 3 - 1, CORE_PARTNER + X_PARTNERS + FAR_X + PLANE_PARTNERS + TURN_PARTNERS
    )(
        body,
        [
            (low, VMEM), (back, VMEM), (residual, VMEM), (tokens, VMEM), (gains, VMEM),
            (second_gain, VMEM), (heads, VMEM), (raw, VMEM), (attended, VMEM), (totals, VMEM),
            (cosine, VMEM), (sine, VMEM), (lengths, VMEM), (qkv, HBM),
            (output, HBM), (normed, HBM), (mlp, HBM), (gate, HBM), (up, HBM), (down, HBM),
        ],
        [
            (shape((128, 2048)), VMEM),
            (shape((128, 2048)), VMEM),
            (shape((128, 512)), VMEM),
            (shape((256, 128)), VMEM),
            (shape((128, 768)), VMEM),
            (shape((128, 768)), VMEM),
            (shape((768, 128)), VMEM),
            (shape((1, 1, 128), F32), VMEM),
        ],
        (
            pltpu.VMEM((1024, 2048), BF16),
            pltpu.VMEM((1024, 2048), BF16),
            pltpu.VMEM((2048, 512), BF16),
            pltpu.VMEM((256, 2048), BF16),
            pltpu.VMEM((2048, 768), BF16),
            pltpu.VMEM((2048, 768), BF16),
            pltpu.VMEM((768, 2048), BF16),
            pltpu.VMEM((2048, 512), BF16),
            pltpu.VMEM((256, 2048), BF16),
            pltpu.VMEM((1024, 256), BF16),
            pltpu.VMEM((1024, 256), BF16),
            pltpu.VMEM((1024, 128), F32),
            pltpu.VMEM((1024, 128), F32),
            pltpu.VMEM((1024, 512), BF16),
            pltpu.VMEM((128, 2048), BF16),
            pltpu.VMEM((128, 2048), BF16),
            pltpu.VMEM((128, 512), BF16),
            pltpu.VMEM((256, 128), BF16),
            pltpu.VMEM((256, 384), BF16),
            pltpu.VMEM((256, 384), BF16),
            pltpu.VMEM((384, 256), BF16),
            pltpu.VMEM((128, 1, 128), F32),
            pltpu.VMEM((127, 1, 128), F32),
        )
        + ROWS_SCRATCH * 2
        + plane_scratch(256, 384) * 2
        + plane_scratch(384, 256)
        + plane_scratch(128, 512)
        + plane_scratch(256, 128),
    )


def step_rates(total_tokens):
    root_tokens = math.sqrt(total_tokens)
    narrow = MODEL_WIDTH ** (-0.5)
    return (
        narrow / (2.0 * root_tokens),
        narrow / (2.0 * root_tokens),
        (QUERY_HEADS * HEAD_SIZE // 128) ** (-0.5) / (0.24 * root_tokens),
        narrow / (0.7 * root_tokens),
        FF ** (-0.5) / (1.2 * root_tokens),
        0.025 / root_tokens,
    )


def update(rows, gradients, state):
    rates = step_rates(GROUP_TOK * 16)

    def kernel(*refs):
        block_, input_, qkv_, output_, gate_, up_, down_, gains_ = refs[:8]
        masters, moments, averages = refs[8:14], refs[14:20], refs[20:26]
        outs = refs[26:]
        outs[0][...] = block_[...]
        outs[1][...] = input_[...]

        def one(n, gradient, spot):
            gradient = gradient.astype(F32)
            moment = MOMENTUM * moments[n][spot] + gradient
            master = masters[n][spot] - rates[n] * (gradient + MOMENTUM * moment)
            outs[2 + n][spot] = master
            outs[8 + n][spot] = moment
            outs[14 + n][spot] = AVERAGING * averages[n][spot] + (1.0 - AVERAGING) * master

        one(0, qkv_[:, 0:256], ...)
        one(1, qkv_[:, 256:384], 0)
        one(1, qkv_[:, 384:512], 1)
        one(2, output_[...], ...)
        one(3, gate_[...], 0)
        one(3, up_[...], 1)
        one(4, down_[...], ...)
        one(5, gains_[0, 0:1, 0:OWN_GAINS], ...)

    outs = [shape(a.shape, a.dtype) for a in rows]
    outs += [shape(a.shape, F32) for a in state]
    arrays = (*rows, *gradients, *state)
    return pl.pallas_call(
        kernel,
        out_shape=outs,
        in_specs=[pl.BlockSpec(memory_space=VMEM)] * len(arrays),
        out_specs=[pl.BlockSpec(memory_space=VMEM)] * len(outs),
        compiler_params=pltpu.CompilerParams(vmem_limit_bytes=61 * 2**20),
        name="update",
    )(*arrays)


def body(tokens, cotangent, doc_lengths, *state):
    query_weight, key_value_weight, output_weight, gateup_weight, down_weight, norm_gains = state[:6]
    cosine, sine = rope_tables()
    (
        residual, tokens_here, cotangent_here, normed, raw, heads, attended, totals,
        cosine, sine, qkv, output, gate, up, down_piece, cotangent_all, gains, lengths,
    ) = attention_forward(
        tokens, cotangent, query_weight, key_value_weight, output_weight, gateup_weight,
        down_weight, norm_gains.reshape(1, OWN_GAINS), doc_lengths,
        jnp.asarray(cosine), jnp.asarray(sine),
    )
    back, low, second_gain, mlp, gate_grad, up_grad, down_grad = feed_forward(
        residual, cotangent_here, gains, cotangent_all, gate, up, down_piece
    )
    block_out, input_grad, *gradients = attention_backward(
        low, back, residual, tokens_here, gains, second_gain, heads, raw, attended, totals,
        cosine, sine, lengths, qkv, output, normed, mlp, gate_grad, up_grad, down_grad,
    )
    state = [a.reshape(1, OWN_GAINS) if a.ndim == 1 else a for a in state]
    outs = update((block_out, input_grad), gradients, state)
    return tuple(a.reshape(OWN_GAINS) if a.shape == (1, OWN_GAINS) else a for a in outs)


def solution(mesh):
    parted = Mesh(mesh.devices.reshape(GRID), AXES)
    data = ("z", "ylo", "core")
    tensor = ("yhi", "x")
    rows = P(AXES, None)
    by_rows = P(data, tensor)
    pair = P(None, data, tensor)
    by_columns = P(tensor, data)
    flat = P(AXES)
    weights = (by_rows, pair, by_columns, pair, by_columns, flat)
    return jax.shard_map(
        body,
        mesh=parted,
        in_specs=(rows, rows, P(data, None)) + weights * 3,
        out_specs=(rows, rows) + weights * 3,
        check_vma=False,
    )
```

profile of v0, /device:TPU:1, one launch (start us, length us, event | category | flops | bytes accessed | tf_op | source)
XLA Modules:
  0.0 261.1 jit_solution(17359418802272319608)
XLA Ops:
  0.7 89.4 %links_0.1 = (f32[128,2048]{1,0:T(8,128)}, bf16[128,2048]{1,0:T(8,128)(2,1)}, bf16[128,2048]{1,0:T(8,128)(2,1)}, bf16[1024,2048]{1,0:T(8,128)(2,1)}, f32[1024,38...) custom-call(bf16[128,2048]{1,0:T(8,128)(2,1)} %refs_0_.1, ...), custom_call_target="tpu_custom_call" | custom-call | tf_op jit(solution)/shard_map/links_0/pallas_call | solution.py:627
  90.1 63.2 %links_1.1 = (f32[128,2048]{1,0:T(8,128)}, bf16[128,2048]{1,0:T(8,128)(2,1)}, f32[1,2048]{1,0:T(1,128)}, bf16[1024,2048]{1,0:T(8,128)(2,1)}, bf16[2048,768]{1,0:...) custom-call(f32[128,2048]{1,0:T(8,128)} %get-tuple-element.73.refs_0_.refs_2_, ...), custom_call_target="tpu_custom_call" | custom-call | tf_op jit(solution)/shard_map/links_1/pallas_call | solution.py:627
  153.2 102.0 %links_2.1 = (bf16[128,2048]{1,0:T(8,128)(2,1)}, bf16[128,2048]{1,0:T(8,128)(2,1)}, bf16[128,512]{1,0:T(8,128)(2,1)}, bf16[256,128]{1,0:T(8,128)(2,1)}, bf16[128...) custom-call(bf16[128,2048]{1,0:T(8,128)(2,1)} %get-tuple-element.80.refs_0_, ...), custom_call_target="tpu_custom_call" | custom-call | tf_op jit(solution)/shard_map/links_2/pallas_call | solution.py:627
  255.2 5.7 %update.1 = (bf16[128,2048]{1,0:T(8,128)(2,1)}, bf16[128,2048]{1,0:T(8,128)(2,1)}, f32[128,256]{1,0:T(8,128)}, f32[2,128,128]{2,1,0:T(8,128)}, f32[256,128]{1,0:...) custom-call(bf16[128,2048]{1,0:T(8,128)(2,1)} %get-tuple-element.98., ...), custom_call_target="tpu_custom_call" | custom-call | tf_op jit(solution)/shard_map/update/pallas_call | solution.py:1557
where the time goes:
time: 261 us
  Pallas kernels  260 us (100%)
    pallas_call x3, Pallas kernels, __call__(): pl.pallas_call(kernel, out_shape=[shape for shape, _ in outs], in_specs=[...  255 us
    pallas_call x1, Pallas kernels, update(): pl.pallas_call(kernel, out_shape=outs, in_specs=[pl.BlockSpec(memory_spac...  5.67 us

commit v1 on v0

--- a/solution.py
+++ b/solution.py
@@ -143,18 +143,19 @@
         return copy
 
 
+def at_step(acts, n):
+    for at, act in (acts or {}).items():
+
+        @pl.when(n == at)
+        def _():
+            act()
+
+
 def staged(count, compute, before=None, after=None):
-    def do(acts, n):
-        for at, act in (acts or {}).items():
-
-            @pl.when(n == at)
-            def _():
-                act()
-
     def step(n, carry):
-        do(before, n)
+        at_step(before, n)
         compute(n)
-        do(after, n)
+        at_step(after, n)
         return carry
 
     lax.fori_loop(0, count, step, 0)
@@ -244,7 +245,7 @@
         self.given = {k: net.into() for k in (0, 1, -1, 2)}
         self.through, self.last = net.into(), net.into()
         net.later(self.passed)
-        net.later(lambda: net.gone(self.along, self.land))
+        net.later(self.departed)
 
     def block(self, core, k, part):
         start = ((self.spots[k] * 2 + core) * 2 + part) * self.half
@@ -262,6 +263,11 @@
         if self.over is not None:
             self.net.gone(self.over, self.landed)
             self.over = None
+
+    def departed(self):
+        if self.along is not None:
+            self.net.gone(self.along, self.land)
+            self.along = None
 
     def combine(self, k):
         self.net.here(self.given[k], self.landed.at[k % RING])
@@ -313,7 +319,13 @@
         self.first = [net.into() for _ in range(2)]
         self.rings = {(color, i): net.into() for color in range(2) for i in (0, 1, -1, -2)}
         self.last = [net.into() for _ in range(2)]
-        net.later(lambda: net.gone(self.out, whole.at[pl.ds(0, whole.shape[0] // 16 * 15)]))
+        net.later(self.gone)
+
+    def gone(self):
+        if self.out is not None:
+            rows = self.whole.shape[0] // 16 * 15
+            self.net.gone(self.out, self.whole.at[pl.ds(0, rows)])
+            self.out = None
 
     def view(self, color, i, j, part=None):
         place = self.net.place
@@ -564,7 +576,7 @@
         for into, axis, count in zip(self.into, ("core", "x", "y", "z"), (1, 2, 8, 32)):
             ways = (1,) if axis == "core" else (1, -1, 2)
             for by in ways:
-                net.send(lambda: (self.spot(axis, 0),) * 2, self.out, into, axis, by)
+                net.send(lambda axis=axis: (self.spot(axis, 0),) * 2, self.out, into, axis, by)
             yield
             net.here(into, self.whole.at[pl.ds(0, count * len(ways))])
         yield
@@ -582,7 +594,7 @@
             ways = (1,) if axis == "core" else (1, -1, 2)
             spots = [pl.ds(first + n * count, count) for n in range(len(ways))]
             for spot, by in zip(spots, ways):
-                refs = lambda spot=spot, by=by: (self.spot(axis, by), land.at[spot])
+                refs = lambda axis=axis, spot=spot, by=by: (self.spot(axis, by), land.at[spot])
                 net.send(refs, self.out, into, axis, by)
             yield
             net.here(into, land.at[pl.ds(first, count * len(ways))])
@@ -631,7 +643,7 @@
             out_specs=[pl.BlockSpec(memory_space=space) for _, space in outs],
             scratch_shapes=[*scratch] + [pltpu.SemaphoreType.DMA((n,)) for n in self.sems],
             compiler_params=pltpu.CompilerParams(
-                collective_id=self.number, has_side_effects=True, vmem_limit_bytes=61 * 2**20
+                collective_id=self.number, has_side_effects=True, vmem_limit_bytes=62 * 2**20
             ),
             name="links_%d" % self.number,
         )(*[array for array, _ in arrays])
@@ -784,14 +796,14 @@
             cosine_, sine_,
         ) = ins
         (
-            residual_, tokens_here, cotangent_here, normed_, raw_, heads_, attended_, totals_,
+            residual_, tokens_here, normed_, raw_, heads_, attended_, totals_,
             cosine_out, sine_out, qkv_out, output_out, gate_out, up_out, down_piece,
             cotangent_all, flat_, lengths_out,
         ) = outs
         (
             gathered, normed, qkv_w, output_w, qkv_cast, output_cast, qkv_piece, output_piece,
             gains_row, gains_rows, lengths_mine, lengths_there, gate_cast, up_cast, down_cast,
-            gate_piece, up_piece, terms, landed, land,
+            gate_piece, up_piece, cotangent_here, terms, landed, land,
         ) = work
         place = net.place
         units = Units(place)
@@ -943,9 +955,9 @@
                 summed = jnp.sum(weights_, axis=-1, keepdims=True)
                 probability = (weights_ * (1.0 / summed)).astype(BF16)
                 attended_[spot, columns] = nn(probability, heads_[0:keys, 384:512]).astype(BF16)
-                totals_[spot, columns] = jnp.broadcast_to(
-                    highest * SCALE + jnp.log(summed), (256, 128)
-                )
+                lane = lax.broadcasted_iota(jnp.int32, (1, 128), 1)
+                ours = (lane >= head * 64) & (lane < head * 64 + 64)
+                totals_[spot] = jnp.where(ours, highest * SCALE + jnp.log(summed), totals_[spot])
 
             staged(2, one)
 
@@ -1012,12 +1024,11 @@
         [
             (shape((128, 2048), F32), VMEM),
             (shape((128, 2048)), VMEM),
-            (shape((128, 2048)), VMEM),
             (shape((1024, 2048)), HBM),
             (shape((1024, 384), F32), VMEM),
             (shape((1024, 512)), VMEM),
             (shape((1024, 256)), VMEM),
-            (shape((1024, 256), F32), VMEM),
+            (shape((1024, 128), F32), VMEM),
             (shape((1024, 128), F32), VMEM),
             (shape((1024, 128), F32), VMEM),
             (shape((2048, 512)), HBM),
@@ -1047,36 +1058,73 @@
             pltpu.VMEM((384, 128), BF16),
             pltpu.VMEM((256, 384), BF16),
             pltpu.VMEM((256, 384), BF16),
+            pltpu.VMEM((128, 2048), BF16),
             pltpu.VMEM((1024, 2048), BF16),
         )
         + ROWS_SCRATCH,
     )
 
 
-def feed_forward(residual, cotangent, gains, cotangent_all, gate, up, down):
+def layer_backward(
+    residual, tokens, gains, lengths, down, cotangent_all, gate, up, heads, raw, attended,
+    totals, cosine, sine, qkv, output, normed,
+):
     def body(net, ins, outs, work):
-        residual_, cotangent_, gains_, cotangent_all_, gate_, up_, down_ = ins
-        back_, low_, gain_grad_, mlp_, gate_grad_, up_grad_, down_grad_ = outs
         (
-            second_low, second, upstream, gate_w, up_w, down_w, hidden, gate_low, up_low, terms,
-            mlp, gate_g, up_g, down_g, landed, land,
+            residual_, tokens_, gains_, lengths_, down_, cotangent_all_, gate_, up_,
+            heads_, raw_, attended_, totals_, cosine_, sine_, qkv_, output_, normed_,
+        ) = ins
+        (
+            block_own, input_own, qkv_own, output_own, gate_own, up_own, down_own, gains_own,
+        ) = outs
+        (
+            low, second, upstream, qkv_w, output_w, gate_w, up_w, down_w, hidden, gate_low, up_low,
+            terms, back_rows, raw_here, totals_here, cosine_here, sine_here, key_sum, value_sum,
+            own_out, qkv_total, output_total, gate_total, up_total, down_total,
+            gain_rows, gain_land, first_gain, flat, landed, land, mlp_landed, mlp_land,
+            gate_land, gate_last, up_land, up_last, down_land, down_last,
+            qkv_land, qkv_last, output_land, output_last, free,
         ) = work
         place = net.place
         units = Units(place)
-        gain = gains_[0:1, 2048:4096]
-        rows = residual_[...]
-        second_low[...] = (rows * inverse_root(rows) * gain).astype(BF16)
-        loads = [
-            net.local(lambda: (gate_, gate_w)),
-            net.local(lambda: (up_, up_w)),
-            net.local(lambda: (cotangent_all_, upstream)),
-        ]
+        mine, theirs = place.core, 1 - place.core
+
+        def load(source, target):
+            return net.local(lambda: (source, target))
+
+        loads = {
+            "gate": load(gate_, gate_w),
+            "up": load(up_, up_w),
+            "upstream": load(cotangent_all_, upstream),
+            "output": load(output_, output_w),
+            "qkv": load(qkv_, qkv_w),
+            "raw": load(raw_, raw_here),
+            "totals": load(totals_, totals_here),
+            "cosine": load(cosine_, cosine_here),
+            "sine": load(sine_, sine_here),
+        }
+        second_gain = gains_[0:1, 2048:4096]
+
+        def second_norm(n):
+            spot = pl.ds(pl.multiple_of(n * 64, 64), 64)
+            rows = residual_[spot]
+            low[spot] = (rows * inverse_root(rows) * second_gain).astype(BF16)
+
+        staged(2, second_norm)
         net.enter()
-        gather = RowsGather(net, second_low, second)
+        gather = RowsGather(net, low, second)
         gather.start()
         down_gather = PlaneGather(net, down_, down_w, down_spot)
         down_gather.start()
         sums = RowsSum(net, terms, landed, land)
+        mlp_sum = RowsSum(net, terms, mlp_landed, mlp_land)
+        first_sum = RowsSum(net, terms, landed, land)
+        last_gather = RowsGather(net, low, upstream)
+        gate_sum = PlaneSum(net, gate_w, gateup_spot, gate_land, gate_last)
+        up_sum = PlaneSum(net, up_w, gateup_spot, up_land, up_last)
+        down_sum = PlaneSum(net, down_w, down_spot, down_land, down_last)
+        qkv_sum = PlaneSum(net, qkv_w, rows_spot, qkv_land, qkv_last)
+        output_sum = PlaneSum(net, output_w, output_spot, output_land, output_last)
 
         def forth(n):
             spot = units.rows(n)
@@ -1088,25 +1136,6 @@
             gate_low[spot] = (upward * (sigmoid + active * (1.0 - sigmoid))).astype(BF16)
             up_low[spot] = active.astype(BF16)
 
-        def begin():
-            loads[0].wait()
-            loads[1].wait()
-            gather.here(0)
-
-        def near():
-            gather.near_first()
-            down_gather.spread()
-            gather.near_second()
-            gather.here(1)
-
-        def far():
-            down_gather.forward()
-            gather.far()
-            gather.here(2)
-
-        staged(4, forth, {0: begin, 1: near, 2: lambda: gather.here(-1), 3: far})
-        down_gather.here()
-
         def back(n):
             spot = units.rows(3 - n)
             hidden_grad = nt(upstream[spot], down_w[...])
@@ -1116,80 +1145,340 @@
                 BF16
             )
 
-        def passed(k, ready=None, go=None):
+        def handed(to, k, ready=None, go=None):
             def act():
-                sums.pass_over(k)
+                to.pass_over(k)
                 if ready is not None:
-                    sums.combine(ready)
+                    to.combine(ready)
                     go()
 
             return act
 
-        loads[2].wait()
-        staged(4, back, None, {
-            0: passed(2),
-            1: passed(-1, 2, sums.start_far),
-            2: passed(1, -1, sums.start_left),
-            3: passed(0, 1, sums.start_right),
-        })
+        def in_turn(to):
+            return {
+                0: handed(to, 2),
+                1: handed(to, -1, 2, to.start_far),
+                2: handed(to, 1, -1, to.start_left),
+                3: handed(to, 0, 1, to.start_right),
+            }
+
+        def begin():
+            for name in ("gate", "up", "upstream"):
+                loads[name].wait()
+            gather.here(0)
+
+        def near():
+            gather.near_first()
+            down_gather.spread()
+            gather.near_second()
+            gather.here(1)
+
+        def far():
+            down_gather.forward()
+            gather.far()
+            gather.here(2)
+
+        staged(4, forth, {0: begin, 1: near, 2: lambda: gather.here(-1), 3: far})
+        down_gather.here()
+        staged(4, back, None, in_turn(sums))
+        sums.combine(0)
+        sums.passed()
+        down_gather.gone()
+
+        def through(n):
+            spot = units.rows(n)
+            terms[spot] = nn(hidden[spot], down_w[...]).astype(BF16)
+
+        staged(4, through, None, {0: sums.forward})
+
         def down_grad(n):
             columns = own_half(256, n)
-            down_g[columns] = tn(hidden[:, columns], upstream[...]).astype(BF16)
-
-        staged(3, down_grad, None, {2: lambda: (sums.combine(0), sums.forward())})
-        stores = [net.local(lambda: (down_g, down_grad_))]
-
-        def weight_grad(low, target):
+            down_w[columns] = tn(hidden[:, columns], upstream[...]).astype(BF16)
+
+        staged(3, down_grad)
+        for axis, by in CORE_PARTNER + X_PARTNERS:
+            pl.semaphore_signal(
+                free, inc=1, device_id=place.device(axis, by), device_id_type=pl.DeviceIdType.MESH
+            )
+        down_sum.start()
+        gather.gone()
+        gain_parts = []
+
+        def own_rows(spot):
+            start = (place.x * 2 + place.core) * 128 + spot.start
+            return pl.ds(pl.multiple_of(start, 64), 64)
+
+        def keep(spot, value):
+            through_, gain_part = norm_back(residual_[spot], second_gain, value)
+            through_ = through_ + upstream[own_rows(spot)].astype(F32)
+            back_rows[spot] = through_
+            low[spot] = through_.astype(BF16)
+            gain_parts.append(jnp.sum(gain_part, axis=0, keepdims=True))
+
+        sums.finish(keep)
+        sums.departed()
+        pl.semaphore_wait(free, 3)
+        last_gather.start()
+
+        def weight_grad(low_grad, target):
             def one(n):
                 columns = own_half(256, n)
-                target[columns] = tn(second[:, columns], low[...]).astype(BF16)
+                target[columns] = tn(second[:, columns], low_grad[...]).astype(BF16)
 
             return one
 
-        staged(8, weight_grad(gate_low, gate_g))
-        stores.append(net.local(lambda: (gate_g, gate_grad_)))
-        gain_parts = []
-
-        def keep(spot, value):
-            through, gain_part = norm_back(residual_[spot], gain, value)
-            through = through + cotangent_[spot].astype(F32)
-            back_[spot] = through
-            low_[spot] = through.astype(BF16)
-            gain_parts.append(jnp.sum(gain_part, axis=0, keepdims=True))
-
-        def through(n):
-            spot = units.rows(n)
-            mlp[spot] = nn(hidden[spot], down_w[...]).astype(BF16)
-
-        staged(4, through)
-        stores.append(net.local(lambda: (mlp, mlp_)))
-        staged(8, weight_grad(up_low, up_g))
-        stores.append(net.local(lambda: (up_g, up_grad_)))
-        sums.finish(keep)
-        gain_grad_[...] = gain_parts[0] + gain_parts[1]
-        for store in stores:
-            store.wait()
-
-    plans = (RowsGather, RowsSum, PlaneGather)
-    return Kernel(1, plans, 0, 0, 3 + 4, CORE_PARTNER + X_PARTNERS + PLANE_PARTNERS)(
+        staged(8, weight_grad(gate_low, gate_w))
+        gate_sum.start()
+        last_gather.near_first()
+        staged(8, weight_grad(up_low, up_w))
+        up_sum.start()
+        heads_cols, attended_cols = hidden.at[:, 0:512], hidden.at[:, 512:768]
+        parts, attended_grad = gate_low.at[:, 0:512], gate_low.at[:, 512:768]
+        attended_rows = up_low.at[:, 0:256]
+        loads["heads"] = load(heads_, heads_cols)
+        loads["attended"] = load(attended_, attended_cols)
+        loads["normed"] = load(normed_, second)
+        for k in (2, 1, -1, 0):
+            mlp_sum.pass_over(k)
+        last_gather.near_second()
+        down_sum.forward()
+        loads["output"].wait()
+
+        def enter(n):
+            grad = nt(upstream[units.rows(n)], output_w[...]).astype(BF16)
+            for core in range(2):
+                attended_grad[units.true_rows(n, core)] = grad[core * 128 : core * 128 + 128]
+
+        def combined():
+            last_gather.here(1)
+            for k in (2, 1, -1, 0):
+                mlp_sum.combine(k)
+
+        def last_far():
+            last_gather.far()
+            mlp_sum.start_far()
+            mlp_sum.start_right()
+            mlp_sum.start_left()
+            last_gather.here(2)
+
+        staged(4, enter, {
+            0: lambda: last_gather.here(0), 1: combined, 2: lambda: last_gather.here(-1), 3: last_far,
+        })
+        loads["heads"].wait()
+        loads["attended"].wait()
+
+        def same_order(n):
+            for core in range(2):
+                start = pl.multiple_of(units.chip(n) * 256 + core * 128, 128)
+                attended_rows[pl.ds(start, 128)] = attended_cols[units.true_rows(n, core)]
+
+        staged(4, same_order)
+
+        def output_grad(n):
+            columns = own_half(512, n)
+            output_w[:, columns] = tn(attended_rows[...], upstream[:, columns]).astype(BF16)
+
+        staged(4, output_grad)
+        output_sum.start()
+        gate_sum.forward()
+        key_sum[...] = jnp.zeros_like(key_sum)
+        value_sum[...] = jnp.zeros_like(value_sum)
+        for name in ("raw", "totals", "cosine", "sine"):
+            loads[name].wait()
+        documents = Documents(lengths_[...])
+        gain_query, gain_key = gains_[0:1, 4096:4224], gains_[0:1, 4224:4352]
+
+        def through_rope(value, spot, raw_part, gain):
+            value = value * cosine_here[spot] + pltpu.roll(value * sine_here[spot], 64, 1)
+            through_, gain_part = norm_back(raw_part, gain, value)
+            return through_.astype(BF16), jnp.sum(gain_part, axis=0, keepdims=True)
+
+        def attend(block, gain_sum):
+            keys = 256 * (block + 1)
+            spot = slice(block * 256, block * 256 + 256)
+
+            def one(head, gain_sum):
+                columns = own_half(128, head)
+                query = hidden[spot, columns]
+                upward = gate_low[spot, pl.ds(pl.multiple_of(512 + head * 128, 128), 128)]
+                key, value = hidden[0:keys, 256:384], hidden[0:keys, 384:512]
+                scores = nt(query, key) * SCALE
+                total = jnp.where(head == 0, totals_here[spot, 0:1], totals_here[spot, 64:65])
+                allowed = allowed_pairs(documents, block * 256, 256, keys)
+                probability = jnp.where(allowed, jnp.exp(scores - total), 0.0)
+                prob_grad = nt(upward, value)
+                centre = jnp.sum(probability * prob_grad, axis=-1, keepdims=True)
+                score_grad = (probability * (prob_grad - centre)).astype(BF16)
+                value_sum[0:keys] += tn(probability.astype(BF16), upward)
+                key_sum[0:keys] += tn(score_grad, query)
+                query_grad = nn(score_grad, key) * SCALE
+                through_, gain_part = through_rope(
+                    query_grad, spot, raw_here[spot, columns], gain_query
+                )
+                for n in range(2):
+                    true = block * 2 + n
+                    start = ((true % RING) * 2 + true // RING) * 128
+                    gate_low[start : start + 128, columns] = through_[n * 128 : n * 128 + 128]
+                return gain_sum + gain_part
+
+            return lax.fori_loop(0, 2, one, gain_sum)
+
+        query_gain = attend(3, jnp.zeros((1, 128), F32))
+        down_sum.gather()
+        query_gain = attend(2, query_gain)
+        mlp_sum.forward()
+        query_gain = attend(1, query_gain)
+        query_gain = attend(0, query_gain)
+        up_sum.forward()
+
+        def key_back(true, gain_sum):
+            spot = pl.ds(pl.multiple_of(true * 128, 128), 128)
+            start = (lax.rem(true, RING) * 2 + lax.div(true, RING)) * 128
+            through_, gain_part = through_rope(
+                key_sum[spot] * SCALE, spot, raw_here[spot, 256:384], gain_key
+            )
+            here = pl.ds(pl.multiple_of(start, 128), 128)
+            gate_low[here, 256:384] = through_
+            gate_low[here, 384:512] = value_sum[spot].astype(BF16)
+            return gain_sum + gain_part
+
+        key_gain = lax.fori_loop(0, 8, key_back, jnp.zeros((1, 128), F32))
+        mlp_sum.passed()
+        last_gather.gone()
+        loads["tokens"] = load(tokens_, low)
+        loads["qkv"].wait()
+        loads["normed"].wait()
+        first_gain[...] = jnp.zeros_like(first_gain)
+
+        def out(n):
+            spot = units.rows(3 - n)
+            value = nt(parts[spot], qkv_w[...])
+            terms[spot] = value.astype(BF16)
+            part = jnp.sum(value * second[spot].astype(F32), axis=0, keepdims=True)
+            first_gain[...] += part
+
+        staged(4, out, None, in_turn(first_sum))
+        gate_sum.gather()
+
+        def qkv_grad(n):
+            columns = own_half(256, n)
+            qkv_w[columns] = tn(second[:, columns], parts[...]).astype(BF16)
+
+        staged(8, qkv_grad, None, {3: lambda: (first_sum.combine(0), first_sum.forward())})
+        qkv_sum.start()
+        flat[...] = jnp.concatenate(
+            [first_gain[...] / gains_[0:1, 0:2048], gain_parts[0] + gain_parts[1], query_gain, key_gain],
+            axis=1,
+        )
+
+        def to_rows(n, total):
+            entry = lax.broadcasted_iota(jnp.int32, (128, 256), 1) + n * 256
+            past = entry - owner_starts((128, 256), 0)
+            here = flat[0:1, own_half(256, n)]
+            owned = jnp.where((past >= 0) & (past < OWN_GAINS), here, 0.0)
+            place_ = lax.broadcasted_iota(jnp.int32, (128, 256), 0)
+            column = (column_of(entry) == place_).astype(F32)
+            return total + lax.dot_general(
+                owned, column, (((1,), (1,)), ((), ())),
+                precision=lax.Precision.HIGHEST, preferred_element_type=F32,
+            )
+
+        rows_of = lax.fori_loop(0, GAINS // 256, to_rows, jnp.zeros((128, 128), F32))
+        gain_rows[...] = rows_of.reshape(128, 1, 128)
+        gains_steps = GainsSum(net, gain_rows, gains_own, gain_land).steps()
+        next(gains_steps)
+        output_sum.forward()
+
+        def keep_block(spot, value):
+            own_out[spot] = (residual_[spot] + value).astype(BF16)
+
+        mlp_sum.finish(keep_block)
+        block_turn = Turn(net, parts_of(own_out, block_own, 2))
+        block_turn.start()
+        next(gains_steps)
+
+        halves = []
+
+        def exchange(cut, there):
+            halves.append(net.local(lambda: (cut(mine), there(mine))))
+            halves.append(
+                Give(net, lambda: (cut(theirs), there(mine)), lambda: there(theirs))
+            )
+
+        down_sum.finish(down_total)
+        exchange(
+            lambda core: down_total.at[:, own_half(128, core)],
+            lambda core: down_own.at[own_half(384, core)],
+        )
+        up_sum.gather()
+        next(gains_steps)
+        output_sum.gather()
+        qkv_sum.forward()
+        next(gains_steps)
+        gate_sum.finish(gate_total)
+        exchange(
+            lambda core: gate_total.at[own_half(128, core)],
+            lambda core: gate_own.at[:, own_half(384, core)],
+        )
+        turns = []
+        block_turn.wait()
+        loads["tokens"].wait()
+
+        def keep_first(spot, value):
+            rows_in = low[spot].astype(F32)
+            through_, _ = norm_back(rows_in, gains_[0:1, 0:2048], value)
+            own_out[spot] = (back_rows[spot] + through_).astype(BF16)
+            turns.append(Turn(net, [(own_out.at[spot], input_own.at[spot])]))
+            turns[-1].start()
+
+        first_sum.finish(keep_first)
+        up_sum.finish(up_total)
+        exchange(
+            lambda core: up_total.at[own_half(128, core)],
+            lambda core: up_own.at[:, own_half(384, core)],
+        )
+        output_sum.finish(output_total)
+        output_turn = Turn(net, [(output_total, output_own)])
+        output_turn.start()
+        qkv_sum.gather()
+        next(gains_steps)
+        qkv_sum.finish(qkv_total)
+        qkv_turn = Turn(net, [(qkv_total, qkv_own)])
+        qkv_turn.start()
+        for copy in halves:
+            copy.wait()
+        for turn in (output_turn, *turns, qkv_turn):
+            turn.wait()
+
+    plans = (
+        2 * (RowsGather,) + 3 * (RowsSum,) + (PlaneGather,) + 5 * (PlaneSum,) + (GainsSum,)
+    )
+    return Kernel(
+        1, plans, 3, 6, 13 + 3 - 1, CORE_PARTNER + X_PARTNERS + FAR_X + PLANE_PARTNERS + TURN_PARTNERS
+    )(
         body,
         [
-            (residual, VMEM), (cotangent, VMEM), (gains, VMEM),
-            (cotangent_all, HBM), (gate, HBM), (up, HBM), (down, VMEM),
+            (residual, VMEM), (tokens, HBM), (gains, VMEM), (lengths, VMEM),
+            (down, VMEM), (cotangent_all, HBM), (gate, HBM), (up, HBM), (heads, HBM), (raw, HBM),
+            (attended, HBM), (totals, HBM), (cosine, HBM), (sine, HBM), (qkv, HBM), (output, HBM),
+            (normed, HBM),
         ],
         [
-            (shape((128, 2048), F32), VMEM),
-            (shape((128, 2048)), VMEM),
-            (shape((1, 2048), F32), VMEM),
-            (shape((1024, 2048)), HBM),
-            (shape((2048, 768)), HBM),
-            (shape((2048, 768)), HBM),
-            (shape((768, 2048)), HBM),
+            (shape((128, 2048)), HBM),
+            (shape((128, 2048)), HBM),
+            (shape((128, 512)), VMEM),
+            (shape((256, 128)), VMEM),
+            (shape((128, 768)), HBM),
+            (shape((128, 768)), HBM),
+            (shape((768, 128)), HBM),
+            (shape((1, 1, 128), F32), VMEM),
         ],
         (
             pltpu.VMEM((128, 2048), BF16),
             pltpu.VMEM((1024, 2048), BF16),
             pltpu.VMEM((1024, 2048), BF16),
+            pltpu.VMEM((2048, 512), BF16),
+            pltpu.VMEM((256, 2048), BF16),
             pltpu.VMEM((2048, 768), BF16),
             pltpu.VMEM((2048, 768), BF16),
             pltpu.VMEM((768, 2048), BF16),
@@ -1197,303 +1486,13 @@
             pltpu.VMEM((1024, 768), BF16),
             pltpu.VMEM((1024, 768), BF16),
             pltpu.VMEM((1024, 2048), BF16),
-            pltpu.VMEM((1024, 2048), BF16),
-            pltpu.VMEM((2048, 768), BF16),
-            pltpu.VMEM((2048, 768), BF16),
-            pltpu.VMEM((768, 2048), BF16),
-        )
-        + ROWS_SCRATCH,
-    )
-
-
-def attention_backward(
-    low, back, residual, tokens, gains, second_gain, heads, raw, attended, totals, cosine, sine,
-    lengths, qkv, output, normed, mlp, gate, up, down,
-):
-    def body(net, ins, outs, work):
-        (
-            low_, back_, residual_, tokens_, gains_, second_gain_, heads_, raw_, attended_, totals_,
-            cosine_, sine_, lengths_, qkv_, output_, normed_, mlp_, gate_, up_, down_,
-        ) = ins
-        (
-            block_own, input_own, qkv_own, output_own, gate_own, up_own, down_own, gains_own,
-        ) = outs
-        (
-            rows, terms, qkv_w, output_w, gate_g, up_g, down_g, qkv_g, output_g,
-            attended_rows, attended_grad, key_sum, value_sum, parts,
-            block_out, input_out, qkv_total, output_total, gate_total, up_total, down_total,
-            gain_rows, gain_land,
-            mlp_landed, mlp_land, first_landed, first_land,
-            gate_land, gate_last, up_land, up_last, down_land, down_last,
-            qkv_land, qkv_last, output_land, output_last,
-        ) = work
-        place = net.place
-        units = Units(place)
-        mine, theirs = place.core, 1 - place.core
-        loads = {
-            name: net.local(lambda source=source, target=target: (source, target))
-            for name, source, target in (
-                ("gate", gate_, gate_g), ("up", up_, up_g), ("output", output_, output_w),
-                ("down", down_, down_g), ("mlp", mlp_, terms), ("qkv", qkv_, qkv_w),
-            )
-        }
-        gather = RowsGather(net, low_, rows)
-        gate_sum = PlaneSum(net, gate_g, gateup_spot, gate_land, gate_last)
-        up_sum = PlaneSum(net, up_g, gateup_spot, up_land, up_last)
-        down_sum = PlaneSum(net, down_g, down_spot, down_land, down_last)
-        qkv_sum = PlaneSum(net, qkv_g, rows_spot, qkv_land, qkv_last)
-        output_sum = PlaneSum(net, output_g, output_spot, output_land, output_last)
-        mlp_sum = RowsSum(net, terms, mlp_landed, mlp_land)
-        first_sum = RowsSum(net, terms, first_landed, first_land)
-
-        def same_order(n):
-            for core in range(2):
-                start = pl.multiple_of(units.chip(n) * 256 + core * 128, 128)
-                attended_rows[pl.ds(start, 128)] = attended_[units.true_rows(n, core)]
-
-        staged(4, same_order)
-        key_sum[...] = jnp.zeros_like(key_sum)
-        value_sum[...] = jnp.zeros_like(value_sum)
-        net.enter()
-        gather.start()
-        loads["gate"].wait()
-        gate_sum.start()
-        loads["up"].wait()
-        up_sum.start()
-        loads["output"].wait()
-
-        halves = []
-
-        def exchange(cut, there):
-            halves.append(net.local(lambda: (cut(mine), there(mine))))
-            halves.append(
-                Give(net, lambda: (cut(theirs), there(mine)), lambda: there(theirs))
-            )
-
-        def enter(n):
-            grad = nt(rows[units.rows(n)], output_w[...]).astype(BF16)
-            for core in range(2):
-                attended_grad[units.true_rows(n, core)] = grad[core * 128 : core * 128 + 128]
-
-        def near():
-            loads["down"].wait()
-            down_sum.start()
-            loads["mlp"].wait()
-            for k in (2, 1, -1, 0):
-                mlp_sum.pass_over(k)
-            gather.near_first()
-            gather.near_second()
-            for k in (2, 1, -1, 0):
-                mlp_sum.combine(k)
-            gather.here(1)
-
-        def far():
-            gather.far()
-            mlp_sum.start_far()
-            mlp_sum.start_right()
-            mlp_sum.start_left()
-            gather.here(2)
-
-        staged(4, enter, {0: lambda: gather.here(0), 1: near, 2: lambda: gather.here(-1), 3: far})
-
-        def output_grad(n):
-            columns = own_half(512, n)
-            output_g[:, columns] = tn(attended_rows[...], rows[:, columns]).astype(BF16)
-
-        staged(4, output_grad)
-        output_sum.start()
-        gate_sum.forward()
-        gather.gone()
-        loads["normed"] = net.local(lambda: (normed_, rows))
-
-        documents = Documents(lengths_[...])
-        gain_query, gain_key = gains_[0:1, 4096:4224], gains_[0:1, 4224:4352]
-
-        def through_rope(value, spot, raw_part, gain):
-            value = value * cosine_[spot] + pltpu.roll(value * sine_[spot], 64, 1)
-            through, gain_part = norm_back(raw_part, gain, value)
-            return through.astype(BF16), jnp.sum(gain_part, axis=0, keepdims=True)
-
-        def attend(block, gain_sum):
-            keys = 256 * (block + 1)
-            spot = slice(block * 256, block * 256 + 256)
-
-            def one(head, gain_sum):
-                columns = own_half(128, head)
-                query, upstream = heads_[spot, columns], attended_grad[spot, columns]
-                key, value = heads_[0:keys, 256:384], heads_[0:keys, 384:512]
-                scores = nt(query, key) * SCALE
-                total = totals_[spot, columns][:, 0:1]
-                allowed = allowed_pairs(documents, block * 256, 256, keys)
-                probability = jnp.where(allowed, jnp.exp(scores - total), 0.0)
-                prob_grad = nt(upstream, value)
-                centre = jnp.sum(probability * prob_grad, axis=-1, keepdims=True)
-                score_grad = (probability * (prob_grad - centre)).astype(BF16)
-                value_sum[0:keys] += tn(probability.astype(BF16), upstream)
-                key_sum[0:keys] += tn(score_grad, query)
-                query_grad = nn(score_grad, key) * SCALE
-                through, gain_part = through_rope(query_grad, spot, raw_[spot, columns], gain_query)
-                for n in range(2):
-                    true = block * 2 + n
-                    start = ((true % RING) * 2 + true // RING) * 128
-                    parts[start : start + 128, columns] = through[n * 128 : n * 128 + 128]
-                return gain_sum + gain_part
-
-            return lax.fori_loop(0, 2, one, gain_sum)
-
-        query_gain = attend(3, jnp.zeros((1, 128), F32))
-        up_sum.forward()
-        mlp_sum.forward()
-        query_gain = attend(2, query_gain)
-        down_sum.forward()
-        query_gain = attend(1, query_gain)
-        query_gain = attend(0, query_gain)
-        gate_sum.gather()
-
-        def keep_block(spot, value):
-            block_out[spot] = (residual_[spot] + value).astype(BF16)
-
-        def key_back(true, gain_sum):
-            spot = pl.ds(pl.multiple_of(true * 128, 128), 128)
-            start = (lax.rem(true, RING) * 2 + lax.div(true, RING)) * 128
-            through, gain_part = through_rope(
-                key_sum[spot] * SCALE, spot, raw_[spot, 256:384], gain_key
-            )
-            here = pl.ds(pl.multiple_of(start, 128), 128)
-            parts[here, 256:384] = through
-            parts[here, 384:512] = value_sum[spot].astype(BF16)
-            return gain_sum + gain_part
-
-        key_gain = lax.fori_loop(0, 8, key_back, jnp.zeros((1, 128), F32))
-        mlp_sum.passed()
-        loads["qkv"].wait()
-
-        def out(n):
-            spot = units.rows(3 - n)
-            terms[spot] = nt(parts[spot], qkv_w[...]).astype(BF16)
-
-        def passed(k, ready=None, go=None):
-            def act():
-                first_sum.pass_over(k)
-                if ready is not None:
-                    first_sum.combine(ready)
-                    go()
-
-            return act
-
-        staged(4, out, None, {
-            0: passed(2),
-            1: passed(-1, 2, first_sum.start_far),
-            2: passed(1, -1, first_sum.start_left),
-            3: passed(0, 1, first_sum.start_right),
-        })
-        loads["normed"].wait()
-
-        def qkv_grad(n):
-            columns = own_half(256, n)
-            qkv_g[columns] = tn(rows[:, columns], parts[...]).astype(BF16)
-
-        staged(8, qkv_grad, None, {3: lambda: (first_sum.combine(0), first_sum.forward())})
-        qkv_sum.start()
-        up_sum.gather()
-        output_sum.forward()
-        down_sum.gather()
-        mlp_sum.finish(keep_block)
-        block_turn = Turn(net, parts_of(block_out, block_own, 2))
-        block_turn.start()
-        gate_sum.finish(gate_total)
-        output_sum.gather()
-        qkv_sum.forward()
-        up_sum.finish(up_total)
-        for source, target in ((gate_total, gate_own), (up_total, up_own)):
-            exchange(
-                lambda core, source=source: source.at[own_half(128, core)],
-                lambda core, target=target: target.at[:, own_half(384, core)],
-            )
-
-        gain_parts = []
-        turns = []
-
-        def keep_first(spot, value):
-            rows_in = tokens_[spot].astype(F32)
-            through, gain_part = norm_back(rows_in, gains_[0:1, 0:2048], value)
-            input_out[spot] = (back_[spot] + through).astype(BF16)
-            gain_parts.append(jnp.sum(gain_part, axis=0, keepdims=True))
-            turns.append(Turn(net, [(input_out.at[spot], input_own.at[spot])]))
-            turns[-1].start()
-
-        first_sum.finish(keep_first)
-        flat = jnp.concatenate(
-            [gain_parts[0] + gain_parts[1], second_gain_[...], query_gain, key_gain], axis=1
-        )
-        entry = lax.broadcasted_iota(jnp.int32, (128, GAINS), 1)
-        past = entry - owner_starts((128, GAINS), 0)
-        owned = jnp.where((past >= 0) & (past < OWN_GAINS), flat, 0.0)
-        column = (column_of(entry) == lax.broadcasted_iota(jnp.int32, (128, GAINS), 0)).astype(F32)
-        gain_rows[...] = lax.dot_general(
-            owned, column, (((1,), (1,)), ((), ())),
-            precision=lax.Precision.HIGHEST, preferred_element_type=F32,
-        ).reshape(128, 1, 128)
-        gains_steps = GainsSum(net, gain_rows, gains_own, gain_land).steps()
-        next(gains_steps)
-        down_sum.finish(down_total)
-        exchange(
-            lambda core: down_total.at[:, own_half(128, core)],
-            lambda core: down_own.at[own_half(384, core)],
-        )
-        output_sum.finish(output_total)
-        output_turn = Turn(net, [(output_total, output_own)])
-        output_turn.start()
-        next(gains_steps)
-        qkv_sum.gather()
-        next(gains_steps)
-        next(gains_steps)
-        qkv_sum.finish(qkv_total)
-        qkv_turn = Turn(net, [(qkv_total, qkv_own)])
-        qkv_turn.start()
-        next(gains_steps)
-        for copy in halves:
-            copy.wait()
-        for turn in (block_turn, output_turn, *turns, qkv_turn):
-            turn.wait()
-
-    plans = (RowsGather,) + 2 * (RowsSum,) + 5 * (PlaneSum,) + (GainsSum,)
-    return Kernel(
-        2, plans, 3, 6, 7 + 3 - 1, CORE_PARTNER + X_PARTNERS + FAR_X + PLANE_PARTNERS + TURN_PARTNERS
-    )(
-        body,
-        [
-            (low, VMEM), (back, VMEM), (residual, VMEM), (tokens, VMEM), (gains, VMEM),
-            (second_gain, VMEM), (heads, VMEM), (raw, VMEM), (attended, VMEM), (totals, VMEM),
-            (cosine, VMEM), (sine, VMEM), (lengths, VMEM), (qkv, HBM),
-            (output, HBM), (normed, HBM), (mlp, HBM), (gate, HBM), (up, HBM), (down, HBM),
-        ],
-        [
-            (shape((128, 2048)), VMEM),
-            (shape((128, 2048)), VMEM),
-            (shape((128, 512)), VMEM),
-            (shape((256, 128)), VMEM),
-            (shape((128, 768)), VMEM),
-            (shape((128, 768)), VMEM),
-            (shape((768, 128)), VMEM),
-            (shape((1, 1, 128), F32), VMEM),
-        ],
-        (
-            pltpu.VMEM((1024, 2048), BF16),
-            pltpu.VMEM((1024, 2048), BF16),
-            pltpu.VMEM((2048, 512), BF16),
-            pltpu.VMEM((256, 2048), BF16),
-            pltpu.VMEM((2048, 768), BF16),
-            pltpu.VMEM((2048, 768), BF16),
-            pltpu.VMEM((768, 2048), BF16),
-            pltpu.VMEM((2048, 512), BF16),
-            pltpu.VMEM((256, 2048), BF16),
-            pltpu.VMEM((1024, 256), BF16),
-            pltpu.VMEM((1024, 256), BF16),
+            pltpu.VMEM((128, 2048), F32),
+            pltpu.VMEM((1024, 384), F32),
             pltpu.VMEM((1024, 128), F32),
             pltpu.VMEM((1024, 128), F32),
-            pltpu.VMEM((1024, 512), BF16),
-            pltpu.VMEM((128, 2048), BF16),
+            pltpu.VMEM((1024, 128), F32),
+            pltpu.VMEM((1024, 128), F32),
+            pltpu.VMEM((1024, 128), F32),
             pltpu.VMEM((128, 2048), BF16),
             pltpu.VMEM((128, 512), BF16),
             pltpu.VMEM((256, 128), BF16),
@@ -1502,12 +1501,15 @@
             pltpu.VMEM((384, 256), BF16),
             pltpu.VMEM((128, 1, 128), F32),
             pltpu.VMEM((127, 1, 128), F32),
+            pltpu.VMEM((1, 2048), F32),
+            pltpu.VMEM((1, GAINS), F32),
         )
         + ROWS_SCRATCH * 2
         + plane_scratch(256, 384) * 2
         + plane_scratch(384, 256)
         + plane_scratch(128, 512)
-        + plane_scratch(256, 128),
+        + plane_scratch(256, 128)
+        + (pltpu.SemaphoreType.REGULAR,),
     )
 
 
@@ -1568,19 +1570,16 @@
     query_weight, key_value_weight, output_weight, gateup_weight, down_weight, norm_gains = state[:6]
     cosine, sine = rope_tables()
     (
-        residual, tokens_here, cotangent_here, normed, raw, heads, attended, totals,
-        cosine, sine, qkv, output, gate, up, down_piece, cotangent_all, gains, lengths,
+        residual, tokens_here, normed, raw, heads, attended, totals,
+        cosine, sine, qkv, output, gate, up, down, cotangent_all, gains, lengths,
     ) = attention_forward(
         tokens, cotangent, query_weight, key_value_weight, output_weight, gateup_weight,
         down_weight, norm_gains.reshape(1, OWN_GAINS), doc_lengths,
         jnp.asarray(cosine), jnp.asarray(sine),
     )
-    back, low, second_gain, mlp, gate_grad, up_grad, down_grad = feed_forward(
-        residual, cotangent_here, gains, cotangent_all, gate, up, down_piece
-    )
-    block_out, input_grad, *gradients = attention_backward(
-        low, back, residual, tokens_here, gains, second_gain, heads, raw, attended, totals,
-        cosine, sine, lengths, qkv, output, normed, mlp, gate_grad, up_grad, down_grad,
+    block_out, input_grad, *gradients = layer_backward(
+        residual, tokens_here, gains, lengths, down, cotangent_all, gate, up,
+        heads, raw, attended, totals, cosine, sine, qkv, output, normed,
     )
     state = [a.reshape(1, OWN_GAINS) if a.ndim == 1 else a for a in state]
     outs = update((block_out, input_grad), gradients, state)

time: 261 us -> 248 us (0.950)
  Pallas kernels: 260 us -> 247 us
    pallas_call x3 -> x2, Pallas kernels: 255 us -> 241 us  [__call__(): pl.pallas_call(kernel, out_shape=[shape for shape, _ in outs], in_specs=[...]
where the time goes in v1:
time: 248 us; the launch traced here: 247 us
  Pallas kernels  247 us (100%)
    pallas_call x2, Pallas kernels, __call__(): pl.pallas_call(kernel, out_shape=[shape for shape, _ in outs], in_specs=[...  241 us
    pallas_call x1, Pallas kernels, update(): pl.pallas_call(kernel, out_shape=outs, in_specs=[pl.BlockSpec(memory_spac...  5.66 us

profile of v1, /device:TPU:1, one launch (start us, length us, event | category | flops | bytes accessed | tf_op | source)
XLA Modules:
  0.0 247.4 jit_solution(13247583780602575760)
XLA Ops:
  0.7 89.2 %links_0.1 = (f32[128,2048]{1,0:T(8,128)}, bf16[128,2048]{1,0:T(8,128)(2,1)}, bf16[1024,2048]{1,0:T(8,128)(2,1)}, f32[1024,384]{1,0:T(8,128)}, bf16[1024,512]{1,...) custom-call(bf16[128,2048]{1,0:T(8,128)(2,1)} %refs_0_.1, ...), custom_call_target="tpu_custom_call" | custom-call | tf_op jit(solution)/shard_map/links_0/pallas_call | solution.py:639
  89.8 151.7 %links_1.1 = (bf16[128,2048]{1,0:T(8,128)(2,1)}, bf16[128,2048]{1,0:T(8,128)(2,1)}, bf16[128,512]{1,0:T(8,128)(2,1)}, bf16[256,128]{1,0:T(8,128)(2,1)}, bf16[128...) custom-call(f32[128,2048]{1,0:T(8,128)} %get-tuple-element.65.refs_0_, ...), custom_call_target="tpu_custom_call" | custom-call | tf_op jit(solution)/shard_map/links_1/pallas_call | solution.py:639
  241.5 5.7 %update.1 = (bf16[128,2048]{1,0:T(8,128)(2,1)}, bf16[128,2048]{1,0:T(8,128)(2,1)}, f32[128,256]{1,0:T(8,128)}, f32[2,128,128]{2,1,0:T(8,128)}, f32[256,128]{1,0:...) custom-call(bf16[128,2048]{1,0:T(8,128)(2,1)} %get-tuple-element.82., ...), custom_call_target="tpu_custom_call" | custom-call | tf_op jit(solution)/shard_map/update/pallas_call | solution.py:1559

commit v2 on v1

--- a/solution.py
+++ b/solution.py
@@ -235,8 +235,9 @@
 class RowsSum:
     OUT, INTO = 2, 6
 
-    def __init__(self, net, whole, landed, land):
+    def __init__(self, net, whole, landed, land, share=0, shares=1):
         self.net, self.whole, self.landed, self.land = net, whole, landed, land
+        self.share, self.shares = share, shares
         self.half = landed.shape[2]
         place = net.place
         self.me, self.other = place.core, 1 - place.core
@@ -248,7 +249,8 @@
         net.later(self.departed)
 
     def block(self, core, k, part):
-        start = ((self.spots[k] * 2 + core) * 2 + part) * self.half
+        block = (self.spots[k] * 2 + core) * self.shares + self.share
+        start = (block * 2 + part) * self.half
         return self.whole.at[pl.ds(pl.multiple_of(start, self.half), self.half)]
 
     def own(self, k, part):
@@ -1081,10 +1083,12 @@
             low, second, upstream, qkv_w, output_w, gate_w, up_w, down_w, hidden, gate_low, up_low,
             terms, back_rows, raw_here, totals_here, cosine_here, sine_here, key_sum, value_sum,
             own_out, qkv_total, output_total, gate_total, up_total, down_total,
-            gain_rows, gain_land, first_gain, flat, landed, land, mlp_landed, mlp_land,
+            gain_rows, gain_land, first_gain, query_gain, flat, landed, land,
             gate_land, gate_last, up_land, up_last, down_land, down_last,
             qkv_land, qkv_last, output_land, output_last, free,
+            early_landed, early_land, late_landed, late_land,
         ) = work
+        share_landed, share_land = (early_landed, late_landed), (early_land, late_land)
         place = net.place
         units = Units(place)
         mine, theirs = place.core, 1 - place.core
@@ -1117,9 +1121,14 @@
         down_gather = PlaneGather(net, down_, down_w, down_spot)
         down_gather.start()
         sums = RowsSum(net, terms, landed, land)
-        mlp_sum = RowsSum(net, terms, mlp_landed, mlp_land)
-        first_sum = RowsSum(net, terms, landed, land)
-        last_gather = RowsGather(net, low, upstream)
+        mlp_sum = RowsSum(net, second, landed, land)
+        first_sums = [
+            RowsSum(
+                net, upstream, share_landed[share], share_land[share], share, 2,
+            )
+            for share in range(2)
+        ]
+        last_gather = RowsGather(net, low, terms)
         gate_sum = PlaneSum(net, gate_w, gateup_spot, gate_land, gate_last)
         up_sum = PlaneSum(net, up_w, gateup_spot, up_land, up_last)
         down_sum = PlaneSum(net, down_w, down_spot, down_land, down_last)
@@ -1136,31 +1145,21 @@
             gate_low[spot] = (upward * (sigmoid + active * (1.0 - sigmoid))).astype(BF16)
             up_low[spot] = active.astype(BF16)
 
+        between = {
+            1: lambda: (sums.combine(2), sums.start_far()),
+            2: lambda: (sums.combine(-1), sums.start_left()),
+            3: lambda: (sums.combine(1), sums.start_right()),
+        }
+
         def back(n):
             spot = units.rows(3 - n)
             hidden_grad = nt(upstream[spot], down_w[...])
             gate_low[spot] = (hidden_grad * gate_low[spot].astype(F32)).astype(BF16)
             up_low[spot] = (hidden_grad * up_low[spot].astype(F32)).astype(BF16)
+            at_step(between, n)
             terms[spot] = (nt(gate_low[spot], gate_w[...]) + nt(up_low[spot], up_w[...])).astype(
                 BF16
             )
-
-        def handed(to, k, ready=None, go=None):
-            def act():
-                to.pass_over(k)
-                if ready is not None:
-                    to.combine(ready)
-                    go()
-
-            return act
-
-        def in_turn(to):
-            return {
-                0: handed(to, 2),
-                1: handed(to, -1, 2, to.start_far),
-                2: handed(to, 1, -1, to.start_left),
-                3: handed(to, 0, 1, to.start_right),
-            }
 
         def begin():
             for name in ("gate", "up", "upstream"):
@@ -1180,29 +1179,32 @@
 
         staged(4, forth, {0: begin, 1: near, 2: lambda: gather.here(-1), 3: far})
         down_gather.here()
-        staged(4, back, None, in_turn(sums))
+        staged(4, back, None, {
+            0: lambda: sums.pass_over(2), 1: lambda: sums.pass_over(-1),
+            2: lambda: sums.pass_over(1), 3: lambda: sums.pass_over(0),
+        })
         sums.combine(0)
         sums.passed()
-        down_gather.gone()
-
-        def through(n):
-            spot = units.rows(n)
-            terms[spot] = nn(hidden[spot], down_w[...]).astype(BF16)
-
-        staged(4, through, None, {0: sums.forward})
-
-        def down_grad(n):
-            columns = own_half(256, n)
-            down_w[columns] = tn(hidden[:, columns], upstream[...]).astype(BF16)
-
-        staged(3, down_grad)
         for axis, by in CORE_PARTNER + X_PARTNERS:
             pl.semaphore_signal(
                 free, inc=1, device_id=place.device(axis, by), device_id_type=pl.DeviceIdType.MESH
             )
-        down_sum.start()
+        sums.forward()
+        gain_parts = []
+
+        def weight_grad(low_grad, target):
+            def one(n):
+                columns = own_half(256, n)
+                target[columns] = tn(second[:, columns], low_grad[...]).astype(BF16)
+
+            return one
+
+        staged(8, weight_grad(gate_low, gate_w))
+        gate_sum.start()
+        staged(8, weight_grad(up_low, up_w))
+        up_sum.start()
         gather.gone()
-        gain_parts = []
+        down_gather.gone()
 
         def own_rows(spot):
             start = (place.x * 2 + place.core) * 128 + spot.start
@@ -1220,41 +1222,92 @@
         pl.semaphore_wait(free, 3)
         last_gather.start()
 
-        def weight_grad(low_grad, target):
-            def one(n):
-                columns = own_half(256, n)
-                target[columns] = tn(second[:, columns], low_grad[...]).astype(BF16)
-
-            return one
-
-        staged(8, weight_grad(gate_low, gate_w))
-        gate_sum.start()
+        def through(n):
+            spot = units.rows(n)
+            second[spot] = nn(hidden[spot], down_w[...]).astype(BF16)
+
+        staged(4, through)
+
+        def down_grad(n):
+            columns = own_half(256, n)
+            down_w[columns] = tn(hidden[:, columns], upstream[...]).astype(BF16)
+
+        staged(3, down_grad)
+        down_sum.start()
         last_gather.near_first()
-        staged(8, weight_grad(up_low, up_w))
-        up_sum.start()
         heads_cols, attended_cols = hidden.at[:, 0:512], hidden.at[:, 512:768]
         parts, attended_grad = gate_low.at[:, 0:512], gate_low.at[:, 512:768]
         attended_rows = up_low.at[:, 0:256]
         loads["heads"] = load(heads_, heads_cols)
         loads["attended"] = load(attended_, attended_cols)
-        loads["normed"] = load(normed_, second)
-        for k in (2, 1, -1, 0):
-            mlp_sum.pass_over(k)
-        last_gather.near_second()
-        down_sum.forward()
+        gate_sum.forward()
         loads["output"].wait()
+        key_sum[...] = jnp.zeros_like(key_sum)
+        value_sum[...] = jnp.zeros_like(value_sum)
+        query_gain[...] = jnp.zeros_like(query_gain)
+        for name in ("heads", "raw", "totals", "cosine", "sine"):
+            loads[name].wait()
+        documents = Documents(lengths_[...])
+        gain_query, gain_key = gains_[0:1, 4096:4224], gains_[0:1, 4224:4352]
+
+        def through_rope(value, cosine_part, sine_part, raw_part, gain):
+            value = value * cosine_part + pltpu.roll(value * sine_part, 64, 1)
+            through_, gain_part = norm_back(raw_part, gain, value)
+            return through_.astype(BF16), jnp.sum(gain_part, axis=0, keepdims=True)
+
+        def twice(value):
+            return jnp.concatenate([value, value], axis=0)
+
+        def both_heads(ref, spot, first):
+            return jnp.concatenate(
+                [ref[spot, first : first + 128], ref[spot, first + 128 : first + 256]], axis=0
+            )
+
+        def attend(n, core):
+            spot = units.true_rows(n, core)
+            keys = 512 * (core + 1)
+            query = both_heads(hidden, spot, 0)
+            upward = both_heads(gate_low, spot, 512)
+            key, value = hidden[0:keys, 256:384], hidden[0:keys, 384:512]
+            scores = nt(query, key) * SCALE
+            total = jnp.concatenate([totals_here[spot, 0:1], totals_here[spot, 64:65]], axis=0)
+            allowed = allowed_pairs(documents, spot.start, 128, keys)
+            probability = jnp.where(twice(allowed), jnp.exp(scores - total), 0.0)
+            prob_grad = nt(upward, value)
+            centre = jnp.sum(probability * prob_grad, axis=-1, keepdims=True)
+            score_grad = (probability * (prob_grad - centre)).astype(BF16)
+            value_sum[0:keys] += tn(probability.astype(BF16), upward)
+            key_sum[0:keys] += tn(score_grad, query)
+            query_grad = nn(score_grad, key) * SCALE
+            through_, gain_part = through_rope(
+                query_grad, twice(cosine_here[spot]), twice(sine_here[spot]),
+                both_heads(raw_here, spot, 0), gain_query,
+            )
+            here = pl.ds(pl.multiple_of(units.chip(n) * 256 + core * 128, 128), 128)
+            gate_low[here, 0:128] = through_[0:128]
+            gate_low[here, 128:256] = through_[128:256]
+            query_gain[...] += gain_part
 
         def enter(n):
-            grad = nt(upstream[units.rows(n)], output_w[...]).astype(BF16)
+            grad = nt(terms[units.rows(n)], output_w[...]).astype(BF16)
             for core in range(2):
                 attended_grad[units.true_rows(n, core)] = grad[core * 128 : core * 128 + 128]
+            for core in range(2):
+                attend(n, core)
+
+        def own_here():
+            last_gather.here(0)
+            for k in (2, 1, -1, 0):
+                mlp_sum.pass_over(k)
 
         def combined():
+            last_gather.near_second()
             last_gather.here(1)
             for k in (2, 1, -1, 0):
                 mlp_sum.combine(k)
 
         def last_far():
+            up_sum.forward()
             last_gather.far()
             mlp_sum.start_far()
             mlp_sum.start_right()
@@ -1262,9 +1315,10 @@
             last_gather.here(2)
 
         staged(4, enter, {
-            0: lambda: last_gather.here(0), 1: combined, 2: lambda: last_gather.here(-1), 3: last_far,
+            0: own_here, 1: combined, 2: lambda: last_gather.here(-1), 3: last_far,
         })
-        loads["heads"].wait()
+        mlp_sum.passed()
+        loads["normed"] = load(normed_, second)
         loads["attended"].wait()
 
         def same_order(n):
@@ -1276,66 +1330,19 @@
 
         def output_grad(n):
             columns = own_half(512, n)
-            output_w[:, columns] = tn(attended_rows[...], upstream[:, columns]).astype(BF16)
+            output_w[:, columns] = tn(attended_rows[...], terms[:, columns]).astype(BF16)
 
         staged(4, output_grad)
         output_sum.start()
-        gate_sum.forward()
-        key_sum[...] = jnp.zeros_like(key_sum)
-        value_sum[...] = jnp.zeros_like(value_sum)
-        for name in ("raw", "totals", "cosine", "sine"):
-            loads[name].wait()
-        documents = Documents(lengths_[...])
-        gain_query, gain_key = gains_[0:1, 4096:4224], gains_[0:1, 4224:4352]
-
-        def through_rope(value, spot, raw_part, gain):
-            value = value * cosine_here[spot] + pltpu.roll(value * sine_here[spot], 64, 1)
-            through_, gain_part = norm_back(raw_part, gain, value)
-            return through_.astype(BF16), jnp.sum(gain_part, axis=0, keepdims=True)
-
-        def attend(block, gain_sum):
-            keys = 256 * (block + 1)
-            spot = slice(block * 256, block * 256 + 256)
-
-            def one(head, gain_sum):
-                columns = own_half(128, head)
-                query = hidden[spot, columns]
-                upward = gate_low[spot, pl.ds(pl.multiple_of(512 + head * 128, 128), 128)]
-                key, value = hidden[0:keys, 256:384], hidden[0:keys, 384:512]
-                scores = nt(query, key) * SCALE
-                total = jnp.where(head == 0, totals_here[spot, 0:1], totals_here[spot, 64:65])
-                allowed = allowed_pairs(documents, block * 256, 256, keys)
-                probability = jnp.where(allowed, jnp.exp(scores - total), 0.0)
-                prob_grad = nt(upward, value)
-                centre = jnp.sum(probability * prob_grad, axis=-1, keepdims=True)
-                score_grad = (probability * (prob_grad - centre)).astype(BF16)
-                value_sum[0:keys] += tn(probability.astype(BF16), upward)
-                key_sum[0:keys] += tn(score_grad, query)
-                query_grad = nn(score_grad, key) * SCALE
-                through_, gain_part = through_rope(
-                    query_grad, spot, raw_here[spot, columns], gain_query
-                )
-                for n in range(2):
-                    true = block * 2 + n
-                    start = ((true % RING) * 2 + true // RING) * 128
-                    gate_low[start : start + 128, columns] = through_[n * 128 : n * 128 + 128]
-                return gain_sum + gain_part
-
-            return lax.fori_loop(0, 2, one, gain_sum)
-
-        query_gain = attend(3, jnp.zeros((1, 128), F32))
-        down_sum.gather()
-        query_gain = attend(2, query_gain)
+        gate_sum.gather()
+        down_sum.forward()
         mlp_sum.forward()
-        query_gain = attend(1, query_gain)
-        query_gain = attend(0, query_gain)
-        up_sum.forward()
-
         def key_back(true, gain_sum):
             spot = pl.ds(pl.multiple_of(true * 128, 128), 128)
             start = (lax.rem(true, RING) * 2 + lax.div(true, RING)) * 128
             through_, gain_part = through_rope(
-                key_sum[spot] * SCALE, spot, raw_here[spot, 256:384], gain_key
+                key_sum[spot] * SCALE, cosine_here[spot], sine_here[spot],
+                raw_here[spot, 256:384], gain_key,
             )
             here = pl.ds(pl.multiple_of(start, 128), 128)
             gate_low[here, 256:384] = through_
@@ -1343,31 +1350,53 @@
             return gain_sum + gain_part
 
         key_gain = lax.fori_loop(0, 8, key_back, jnp.zeros((1, 128), F32))
-        mlp_sum.passed()
         last_gather.gone()
         loads["tokens"] = load(tokens_, low)
         loads["qkv"].wait()
         loads["normed"].wait()
+        up_sum.gather()
         first_gain[...] = jnp.zeros_like(first_gain)
 
         def out(n):
             spot = units.rows(3 - n)
             value = nt(parts[spot], qkv_w[...])
-            terms[spot] = value.astype(BF16)
+            upstream[spot] = value.astype(BF16)
             part = jnp.sum(value * second[spot].astype(F32), axis=0, keepdims=True)
             first_gain[...] += part
 
-        staged(4, out, None, in_turn(first_sum))
-        gate_sum.gather()
+        early, late = first_sums
+
+        def give(k):
+            for one in first_sums:
+                one.pass_over(k)
+
+        staged(4, out, None, {
+            0: lambda: give(2),
+            1: lambda: (give(-1), early.combine(2), early.start_far()),
+            2: lambda: (give(1), early.combine(-1), early.start_left()),
+            3: lambda: (give(0), early.combine(1), early.start_right()),
+        })
+        output_sum.forward()
+
+        def keep_block(spot, value):
+            own_out[spot] = (residual_[spot] + value).astype(BF16)
+
+        mlp_sum.finish(keep_block)
+        block_turn = Turn(net, parts_of(own_out, block_own, 2))
+        block_turn.start()
 
         def qkv_grad(n):
             columns = own_half(256, n)
             qkv_w[columns] = tn(second[:, columns], parts[...]).astype(BF16)
 
-        staged(8, qkv_grad, None, {3: lambda: (first_sum.combine(0), first_sum.forward())})
+        staged(8, qkv_grad, None, {
+            1: lambda: (late.combine(2), late.start_far(), early.combine(0)),
+            3: lambda: (early.forward(), late.combine(-1), late.start_left()),
+            5: lambda: (late.combine(1), late.start_right(), late.combine(0)),
+        })
         qkv_sum.start()
         flat[...] = jnp.concatenate(
-            [first_gain[...] / gains_[0:1, 0:2048], gain_parts[0] + gain_parts[1], query_gain, key_gain],
+            [first_gain[...] / gains_[0:1, 0:2048], gain_parts[0] + gain_parts[1], query_gain[...], key_gain],
             axis=1,
         )
 
@@ -1385,16 +1414,8 @@
 
         rows_of = lax.fori_loop(0, GAINS // 256, to_rows, jnp.zeros((128, 128), F32))
         gain_rows[...] = rows_of.reshape(128, 1, 128)
+        late.forward()
         gains_steps = GainsSum(net, gain_rows, gains_own, gain_land).steps()
-        next(gains_steps)
-        output_sum.forward()
-
-        def keep_block(spot, value):
-            own_out[spot] = (residual_[spot] + value).astype(BF16)
-
-        mlp_sum.finish(keep_block)
-        block_turn = Turn(net, parts_of(own_out, block_own, 2))
-        block_turn.start()
         next(gains_steps)
 
         halves = []
@@ -1405,53 +1426,59 @@
                 Give(net, lambda: (cut(theirs), there(mine)), lambda: there(theirs))
             )
 
+        output_sum.gather()
+        qkv_sum.forward()
+        next(gains_steps)
+        down_sum.gather()
+        gate_sum.finish(gate_total)
+        exchange(
+            lambda core: gate_total.at[own_half(128, core)],
+            lambda core: gate_own.at[:, own_half(384, core)],
+        )
+        output_sum.finish(output_total)
+        output_turn = Turn(net, [(output_total, output_own)])
+        output_turn.start()
+        next(gains_steps)
+        turns = []
+        block_turn.wait()
+        loads["tokens"].wait()
+
+        def ended(share):
+            def keep_first(spot, value):
+                spot = pl.ds(64 * share + spot.start, 32)
+                through_, _ = norm_back(low[spot].astype(F32), gains_[0:1, 0:2048], value)
+                own_out[spot] = (back_rows[spot] + through_).astype(BF16)
+
+            first_sums[share].finish(keep_first)
+            spot = pl.ds(64 * share, 64)
+            turns.append(Turn(net, [(own_out.at[spot], input_own.at[spot])]))
+            turns[-1].start()
+
+        ended(0)
+        qkv_sum.gather()
+        next(gains_steps)
+        ended(1)
+        qkv_sum.finish(qkv_total)
+        qkv_turn = Turn(net, [(qkv_total, qkv_own)])
+        qkv_turn.start()
+        up_sum.finish(up_total)
+        exchange(
+            lambda core: up_total.at[own_half(128, core)],
+            lambda core: up_own.at[:, own_half(384, core)],
+        )
         down_sum.finish(down_total)
         exchange(
             lambda core: down_total.at[:, own_half(128, core)],
             lambda core: down_own.at[own_half(384, core)],
         )
-        up_sum.gather()
         next(gains_steps)
-        output_sum.gather()
-        qkv_sum.forward()
-        next(gains_steps)
-        gate_sum.finish(gate_total)
-        exchange(
-            lambda core: gate_total.at[own_half(128, core)],
-            lambda core: gate_own.at[:, own_half(384, core)],
-        )
-        turns = []
-        block_turn.wait()
-        loads["tokens"].wait()
-
-        def keep_first(spot, value):
-            rows_in = low[spot].astype(F32)
-            through_, _ = norm_back(rows_in, gains_[0:1, 0:2048], value)
-            own_out[spot] = (back_rows[spot] + through_).astype(BF16)
-            turns.append(Turn(net, [(own_out.at[spot], input_own.at[spot])]))
-            turns[-1].start()
-
-        first_sum.finish(keep_first)
-        up_sum.finish(up_total)
-        exchange(
-            lambda core: up_total.at[own_half(128, core)],
-            lambda core: up_own.at[:, own_half(384, core)],
-        )
-        output_sum.finish(output_total)
-        output_turn = Turn(net, [(output_total, output_own)])
-        output_turn.start()
-        qkv_sum.gather()
-        next(gains_steps)
-        qkv_sum.finish(qkv_total)
-        qkv_turn = Turn(net, [(qkv_total, qkv_own)])
-        qkv_turn.start()
         for copy in halves:
             copy.wait()
         for turn in (output_turn, *turns, qkv_turn):
             turn.wait()
 
     plans = (
-        2 * (RowsGather,) + 3 * (RowsSum,) + (PlaneGather,) + 5 * (PlaneSum,) + (GainsSum,)
+        2 * (RowsGather,) + 4 * (RowsSum,) + (PlaneGather,) + 5 * (PlaneSum,) + (GainsSum,)
     )
     return Kernel(
         1, plans, 3, 6, 13 + 3 - 1, CORE_PARTNER + X_PARTNERS + FAR_X + PLANE_PARTNERS + TURN_PARTNERS
@@ -1502,14 +1529,16 @@
             pltpu.VMEM((128, 1, 128), F32),
             pltpu.VMEM((127, 1, 128), F32),
             pltpu.VMEM((1, 2048), F32),
+            pltpu.VMEM((1, 128), F32),
             pltpu.VMEM((1, GAINS), F32),
         )
-        + ROWS_SCRATCH * 2
+        + ROWS_SCRATCH
         + plane_scratch(256, 384) * 2
         + plane_scratch(384, 256)
         + plane_scratch(128, 512)
         + plane_scratch(256, 128)
-        + (pltpu.SemaphoreType.REGULAR,),
+        + (pltpu.SemaphoreType.REGULAR,)
+        + (pltpu.VMEM((4, 2, 32, 2048), BF16), pltpu.VMEM((6, 32, 2048), BF16)) * 2,
     )
 
 

time: 248 us -> 239 us (0.964)
  Pallas kernels: 247 us -> 235 us
    pallas_call x2, Pallas kernels: 241 us -> 230 us  [__call__(): pl.pallas_call(kernel, out_shape=[shape for shape, _ in outs], in_specs=[...]
where the time goes in v2:
time: 239 us; the launch traced here: 236 us
  Pallas kernels  235 us (98%)
    pallas_call x2, Pallas kernels, __call__(): pl.pallas_call(kernel, out_shape=[shape for shape, _ in outs], in_specs=[...  230 us
    pallas_call x1, Pallas kernels, update(): pl.pallas_call(kernel, out_shape=outs, in_specs=[pl.BlockSpec(memory_spac...  5.66 us

profile of v2, /device:TPU:1, one launch (start us, length us, event | category | flops | bytes accessed | tf_op | source)
XLA Modules:
  0.0 236.3 jit_solution(16019783603793314365)
XLA Ops:
  0.7 89.2 %links_0.1 = (f32[128,2048]{1,0:T(8,128)}, bf16[128,2048]{1,0:T(8,128)(2,1)}, bf16[1024,2048]{1,0:T(8,128)(2,1)}, f32[1024,384]{1,0:T(8,128)}, bf16[1024,512]{1,...) custom-call(bf16[128,2048]{1,0:T(8,128)(2,1)} %refs_0_.1, ...), custom_call_target="tpu_custom_call" | custom-call | tf_op jit(solution)/shard_map/links_0/pallas_call | solution.py:641
  89.8 140.6 %links_1.1 = (bf16[128,2048]{1,0:T(8,128)(2,1)}, bf16[128,2048]{1,0:T(8,128)(2,1)}, bf16[128,512]{1,0:T(8,128)(2,1)}, bf16[256,128]{1,0:T(8,128)(2,1)}, bf16[128...) custom-call(f32[128,2048]{1,0:T(8,128)} %get-tuple-element.65.refs_0_, ...), custom_call_target="tpu_custom_call" | custom-call | tf_op jit(solution)/shard_map/links_1/pallas_call | solution.py:641
  230.5 5.7 %update.1 = (bf16[128,2048]{1,0:T(8,128)(2,1)}, bf16[128,2048]{1,0:T(8,128)(2,1)}, f32[128,256]{1,0:T(8,128)}, f32[2,128,128]{2,1,0:T(8,128)}, f32[256,128]{1,0:...) custom-call(bf16[128,2048]{1,0:T(8,128)(2,1)} %get-tuple-element.82., ...), custom_call_target="tpu_custom_call" | custom-call | tf_op jit(solution)/shard_map/update/pallas_call | solution.py:1588

commit v3 on v2

--- a/solution.py
+++ b/solution.py
@@ -312,10 +312,11 @@
 class PlaneGather:
     OUT, INTO, LOCALS = 1, 12, 1
 
-    def __init__(self, net, own, whole, spot):
+    def __init__(self, net, own, whole, spot, first_rows=None):
         self.net, self.own, self.whole, self.spot = net, own, whole, spot
         self.rows = own.shape[0]
-        self.half = self.rows // 2
+        first_rows = self.rows // 2 if first_rows is None else first_rows
+        self.sizes, self.starts = (first_rows, self.rows - first_rows), (0, first_rows)
         self.width = own.shape[1]
         self.out = net.out()
         self.first = [net.into() for _ in range(2)]
@@ -334,21 +335,24 @@
         first, second = self.axes(color)
         a, b = place.step(first, i), place.step(second, j)
         row, columns = self.spot(a, b) if color == 0 else self.spot(b, a)
-        start = row + color * self.half
-        if part is None:
-            return self.whole.at[pl.ds(pl.multiple_of(start, self.half), self.half), columns]
-        size = self.half // 2
-        return self.whole.at[pl.ds(pl.multiple_of(start + part * size, size), size), columns]
-
-    def bytes_of(self, halves):
-        return self.whole.at[pl.ds(0, halves * self.half), pl.ds(0, self.width)]
+        start, size = row + self.starts[color], self.sizes[color]
+        if part is not None:
+            size //= 2
+            start = start + part * size
+        return self.whole.at[pl.ds(pl.multiple_of(start, math.gcd(size, self.rows)), size), columns]
+
+    def bytes_of(self, color, count):
+        size = self.sizes[color]
+        if count * size <= self.whole.shape[0]:
+            return self.whole.at[pl.ds(0, count * size), pl.ds(0, self.width)]
+        return self.whole.at[pl.ds(0, size), pl.ds(0, count * self.width)]
 
     @staticmethod
     def axes(color):
         return ("z", "y") if color == 0 else ("y", "z")
 
     def mine(self, color):
-        return self.own.at[pl.ds(color * self.half, self.half)]
+        return self.own.at[pl.ds(self.starts[color], self.sizes[color])]
 
     def ring(self, color, i):
         axis = self.axes(color)[1]
@@ -374,22 +378,16 @@
 
     def spread(self):
         for color in range(2):
-            self.net.here(self.first[color], self.bytes_of(3) if self.fits(3) else self.thin(3))
+            self.net.here(self.first[color], self.bytes_of(color, 3))
         for i in (-1, 1, -2):
             for color in range(2):
                 self.ring(color, i)
-
-    def fits(self, halves):
-        return halves * self.half <= self.whole.shape[0]
-
-    def thin(self, halves):
-        return self.whole.at[pl.ds(0, self.half), pl.ds(0, halves * self.width)]
 
     def forward(self, steps=(0, 1, -1, -2)):
         for i in steps:
             for color in range(2):
                 axis = self.axes(color)[1]
-                self.net.here(self.rings[color, i], self.bytes_of(2))
+                self.net.here(self.rings[color, i], self.bytes_of(color, 2))
                 for j, part, by in ((-1, 0, 1), (1, 1, -1)):
                     refs = lambda color=color, i=i, j=j, part=part: (
                         self.view(color, i, j, part),
@@ -398,23 +396,26 @@
 
     def here(self):
         for color in range(2):
-            self.net.here(self.last[color], self.bytes_of(4) if self.fits(4) else self.thin(4))
+            self.net.here(self.last[color], self.bytes_of(color, 4))
         self.kept.wait()
 
 
 class PlaneSum:
-    OUT, INTO = 2, 18
-
-    def __init__(self, net, whole, spot, land, last):
-        self.net, self.whole, self.spot, self.land, self.last = net, whole, spot, land, last
-        self.size = land.shape[3]
-        self.ring_out, self.last_out = net.out(), net.out()
+    OUT, INTO = 4, 18
+
+    def __init__(self, net, whole, spot, scratch):
+        self.net, self.whole, self.spot = net, whole, spot
+        self.land, self.last = scratch[0:2], scratch[2:4]
+        self.sizes = [land.shape[2] for land in self.land]
+        self.starts = (0, 2 * self.sizes[0])
+        self.ring_out, self.last_out = (net.out(), net.out()), (net.out(), net.out())
         ways = [(color, k) for color in range(2) for k in range(RING)]
         self.through = {way: net.into() for way in ways}
         self.sides = {way: net.into() for way in ways}
         self.ends = [net.into() for _ in range(2)]
-        net.later(lambda: net.gone(self.ring_out, land))
-        net.later(lambda: net.gone(self.last_out, last))
+        for color in range(2):
+            net.later(lambda color=color: net.gone(self.ring_out[color], self.land[color]))
+            net.later(lambda color=color: net.gone(self.last_out[color], self.last[color]))
 
     @staticmethod
     def axes(color):
@@ -425,14 +426,15 @@
         first, second = self.axes(color)
         a, b = place.step(first, n), place.step(second, k)
         row, columns = self.spot(b, a) if color == 0 else self.spot(a, b)
-        start = row + (color * 2 + part) * self.size
-        return self.whole.at[pl.ds(pl.multiple_of(start, self.size), self.size), columns]
+        size = self.sizes[color]
+        start = row + self.starts[color] + part * size
+        return self.whole.at[pl.ds(pl.multiple_of(start, math.gcd(size, 128)), size), columns]
 
     def slot(self, color, k, n):
-        return self.land.at[color, k % RING, n]
+        return self.land[color].at[k % RING, n]
 
     def end(self, color, k, part):
-        return self.last.at[color, k % RING - 1, part]
+        return self.last[color].at[k % RING - 1, part]
 
     def start(self):
         for k in (2, 1, -1, 0):
@@ -446,7 +448,7 @@
                     refs = lambda color=color, k=k, n=n, part=part, slot=slot: (
                         self.own(color, n, k, part), self.slot(color, k, slot)
                     )
-                    self.net.send(refs, self.ring_out, into, axis, by)
+                    self.net.send(refs, self.ring_out[color], into, axis, by)
 
     def forward(self, steps=(2, 1, -1, 0)):
         for k in steps:
@@ -454,7 +456,7 @@
                 axis = self.axes(color)[0]
                 sides = self.sides[color, k % RING]
                 self.net.here(
-                    self.through[color, k % RING], self.land.at[color, k % RING, pl.ds(0, 2)]
+                    self.through[color, k % RING], self.land[color].at[k % RING, pl.ds(0, 2)]
                 )
                 for slot, n, part, target, by in ((0, 1, 0, 2, 1), (1, -1, 1, 5, -1)):
                     here = self.slot(color, k, slot)
@@ -462,14 +464,14 @@
                     refs = lambda color=color, k=k, slot=slot, target=target: (
                         self.slot(color, k, slot), self.slot(color, k, target)
                     )
-                    self.net.send(refs, self.ring_out, sides, axis, by)
+                    self.net.send(refs, self.ring_out[color], sides, axis, by)
 
     def gather(self, steps=(2, 1, -1, 0)):
         for k in steps:
             for color in range(2):
                 second = self.axes(color)[1]
                 self.net.here(
-                    self.sides[color, k % RING], self.land.at[color, k % RING, pl.ds(2, 4)]
+                    self.sides[color, k % RING], self.land[color].at[k % RING, pl.ds(2, 4)]
                 )
                 for part in range(2):
                     here = self.slot(color, k, 2 + part)
@@ -480,23 +482,24 @@
                         refs = lambda color=color, k=k, part=part: (
                             self.slot(color, k, 2 + part), self.end(color, k, part)
                         )
-                        self.net.send(refs, self.last_out, self.ends[color], second, k)
+                        self.net.send(refs, self.last_out[color], self.ends[color], second, k)
 
     def finish(self, total):
         for color in range(2):
-            self.net.here(self.ends[color], self.last.at[color])
+            self.net.here(self.ends[color], self.last[color])
             for part in range(2):
                 value = self.slot(color, 0, 2 + part)[...].astype(F32)
                 for k in (1, -1, 2):
                     value = value + self.end(color, k, part)[...].astype(F32)
-                start = (color * 2 + part) * self.size
-                total[pl.ds(start, self.size)] = value.astype(total.dtype)
-
-
-def plane_scratch(rows, columns):
-    return (
-        pltpu.VMEM((2, 4, 6, rows // 4, columns), BF16),
-        pltpu.VMEM((2, 3, 2, rows // 4, columns), BF16),
+                start = self.starts[color] + part * self.sizes[color]
+                total[pl.ds(start, self.sizes[color])] = value.astype(total.dtype)
+
+
+def plane_scratch(rows, columns, first_rows=None):
+    first_rows = rows // 2 if first_rows is None else first_rows
+    parts = (first_rows // 2, (rows - first_rows) // 2)
+    return tuple(
+        pltpu.VMEM((*dims, part, columns), BF16) for dims in ((4, 6), (3, 2)) for part in parts
     )
 
 
@@ -798,14 +801,15 @@
             cosine_, sine_,
         ) = ins
         (
-            residual_, tokens_here, normed_, raw_, heads_, attended_, totals_,
-            cosine_out, sine_out, qkv_out, output_out, gate_out, up_out, down_piece,
+            residual_, tokens_here, normed_, raw_hbm, heads_hbm, attended_hbm, totals_hbm,
+            cosine_hbm, sine_hbm, qkv_out, output_out, gate_out, up_out, down_piece,
             cotangent_all, flat_, lengths_out,
         ) = outs
         (
             gathered, normed, qkv_w, output_w, qkv_cast, output_cast, qkv_piece, output_piece,
             gains_row, gains_rows, lengths_mine, lengths_there, gate_cast, up_cast, down_cast,
-            gate_piece, up_piece, cotangent_here, terms, landed, land,
+            gate_piece, up_piece, cotangent_here, terms, raw_, heads_, attended_, totals_,
+            cosine_out, sine_out, landed, land,
         ) = work
         place = net.place
         units = Units(place)
@@ -827,8 +831,8 @@
         qkv_turn.start()
         for part in rows:
             part.start()
-        qkv_gather = PlaneGather(net, qkv_piece, qkv_w, rows_spot)
-        output_gather = PlaneGather(net, output_piece, output_w, output_spot)
+        qkv_gather = PlaneGather(net, qkv_piece, qkv_w, rows_spot, 32)
+        output_gather = PlaneGather(net, output_piece, output_w, output_spot, 64)
         gate_gather = PlaneGather(net, gate_piece, gate_out, gateup_spot)
         up_gather = PlaneGather(net, up_piece, up_out, gateup_spot)
         gather = RowsGather(net, tokens_here, gathered)
@@ -965,12 +969,12 @@
 
         attend(0)
         attend(1)
-        later.near_first()
-        up_gather.spread()
         attend(2)
         output_gather.here()
         stores.append(net.local(lambda: (output_w, output_out)))
         attend(3)
+        later.near_first()
+        up_gather.spread()
         sums = RowsSum(net, terms, landed, land)
 
         def out(n):
@@ -989,17 +993,22 @@
 
             return act
 
-        later.near_second()
         staged(4, out, None, {
             0: passed(2),
             1: passed(-1, 2, sums.start_far),
             2: passed(1, -1, sums.start_left),
             3: passed(0, 1, sums.start_right),
         })
-        later.far()
-        gate_gather.forward()
+        for source, target in (
+            (raw_, raw_hbm), (heads_, heads_hbm), (attended_, attended_hbm),
+            (totals_, totals_hbm), (cosine_out, cosine_hbm), (sine_out, sine_hbm),
+        ):
+            stores.append(net.local(lambda source=source, target=target: (source, target)))
         sums.combine(0)
         sums.forward()
+        later.near_second()
+        gate_gather.forward()
+        later.far()
         up_gather.forward()
         for k in (0, 1, -1, 2):
             later.here(k)
@@ -1015,7 +1024,7 @@
 
     plans = (GainsGather,) + 4 * (PlaneGather,) + 2 * (RowsGather,) + (RowsSum,)
     return Kernel(
-        0, plans, 4, 6, 3, CORE_PARTNER + X_PARTNERS + FAR_X + PLANE_PARTNERS + TURN_PARTNERS
+        0, plans, 4, 6, 9, CORE_PARTNER + X_PARTNERS + FAR_X + PLANE_PARTNERS + TURN_PARTNERS
     )(
         body,
         [
@@ -1027,12 +1036,12 @@
             (shape((128, 2048), F32), VMEM),
             (shape((128, 2048)), VMEM),
             (shape((1024, 2048)), HBM),
-            (shape((1024, 384), F32), VMEM),
-            (shape((1024, 512)), VMEM),
-            (shape((1024, 256)), VMEM),
-            (shape((1024, 128), F32), VMEM),
-            (shape((1024, 128), F32), VMEM),
-            (shape((1024, 128), F32), VMEM),
+            (shape((1024, 384), F32), HBM),
+            (shape((1024, 512)), HBM),
+            (shape((1024, 256)), HBM),
+            (shape((1024, 128), F32), HBM),
+            (shape((1024, 128), F32), HBM),
+            (shape((1024, 128), F32), HBM),
             (shape((2048, 512)), HBM),
             (shape((256, 2048)), HBM),
             (shape((2048, 768)), HBM),
@@ -1062,6 +1071,12 @@
             pltpu.VMEM((256, 384), BF16),
             pltpu.VMEM((128, 2048), BF16),
             pltpu.VMEM((1024, 2048), BF16),
+            pltpu.VMEM((1024, 384), F32),
+            pltpu.VMEM((1024, 512), BF16),
+            pltpu.VMEM((1024, 256), BF16),
+            pltpu.VMEM((1024, 128), F32),
+            pltpu.VMEM((1024, 128), F32),
+            pltpu.VMEM((1024, 128), F32),
         )
         + ROWS_SCRATCH,
     )
@@ -1084,8 +1099,7 @@
             terms, back_rows, raw_here, totals_here, cosine_here, sine_here, key_sum, value_sum,
             own_out, qkv_total, output_total, gate_total, up_total, down_total,
             gain_rows, gain_land, first_gain, query_gain, flat, landed, land,
-            gate_land, gate_last, up_land, up_last, down_land, down_last,
-            qkv_land, qkv_last, output_land, output_last, free,
+            *planes, free,
             early_landed, early_land, late_landed, late_land,
         ) = work
         share_landed, share_land = (early_landed, late_landed), (early_land, late_land)
@@ -1129,11 +1143,11 @@
             for share in range(2)
         ]
         last_gather = RowsGather(net, low, terms)
-        gate_sum = PlaneSum(net, gate_w, gateup_spot, gate_land, gate_last)
-        up_sum = PlaneSum(net, up_w, gateup_spot, up_land, up_last)
-        down_sum = PlaneSum(net, down_w, down_spot, down_land, down_last)
-        qkv_sum = PlaneSum(net, qkv_w, rows_spot, qkv_land, qkv_last)
-        output_sum = PlaneSum(net, output_w, output_spot, output_land, output_last)
+        gate_sum = PlaneSum(net, gate_w, gateup_spot, planes[0:4])
+        up_sum = PlaneSum(net, up_w, gateup_spot, planes[4:8])
+        down_sum = PlaneSum(net, down_w, down_spot, planes[8:12])
+        qkv_sum = PlaneSum(net, qkv_w, rows_spot, planes[12:16])
+        output_sum = PlaneSum(net, output_w, output_spot, planes[16:20])
 
         def forth(n):
             spot = units.rows(n)
@@ -1535,8 +1549,8 @@
         + ROWS_SCRATCH
         + plane_scratch(256, 384) * 2
         + plane_scratch(384, 256)
-        + plane_scratch(128, 512)
-        + plane_scratch(256, 128)
+        + plane_scratch(128, 512, 32)
+        + plane_scratch(256, 128, 64)
         + (pltpu.SemaphoreType.REGULAR,)
         + (pltpu.VMEM((4, 2, 32, 2048), BF16), pltpu.VMEM((6, 32, 2048), BF16)) * 2,
     )

time: 239 us -> 235 us (0.983)
  no operation moved by 1% of the time
where the time goes in v3:
time: 235 us; the launch traced here: 234 us
  Pallas kernels  233 us (99%)
    pallas_call x2, Pallas kernels, __call__(): pl.pallas_call(kernel, out_shape=[shape for shape, _ in outs], in_specs=[...  227 us
    pallas_call x1, Pallas kernels, update(): pl.pallas_call(kernel, out_shape=outs, in_specs=[pl.BlockSpec(memory_spac...  5.66 us

profile of v3, /device:TPU:1, one launch (start us, length us, event | category | flops | bytes accessed | tf_op | source)
XLA Modules:
  0.0 233.9 jit_solution(5315110516583142391)
XLA Ops:
  0.7 84.6 %links_0.1 = (f32[128,2048]{1,0:T(8,128)}, bf16[128,2048]{1,0:T(8,128)(2,1)}, bf16[1024,2048]{1,0:T(8,128)(2,1)}, f32[1024,384]{1,0:T(8,128)}, bf16[1024,512]{1,...) custom-call(bf16[128,2048]{1,0:T(8,128)(2,1)} %refs_0_.1, ...), custom_call_target="tpu_custom_call" | custom-call | tf_op jit(solution)/shard_map/links_0/pallas_call | solution.py:644
  85.2 142.8 %links_1.1 = (bf16[128,2048]{1,0:T(8,128)(2,1)}, bf16[128,2048]{1,0:T(8,128)(2,1)}, bf16[128,512]{1,0:T(8,128)(2,1)}, bf16[256,128]{1,0:T(8,128)(2,1)}, bf16[128...) custom-call(f32[128,2048]{1,0:T(8,128)} %get-tuple-element.65.refs_0_, ...), custom_call_target="tpu_custom_call" | custom-call | tf_op jit(solution)/shard_map/links_1/pallas_call | solution.py:644
  228.1 5.7 %update.1 = (bf16[128,2048]{1,0:T(8,128)(2,1)}, bf16[128,2048]{1,0:T(8,128)(2,1)}, f32[128,256]{1,0:T(8,128)}, f32[2,128,128]{2,1,0:T(8,128)}, f32[256,128]{1,0:...) custom-call(bf16[128,2048]{1,0:T(8,128)(2,1)} %get-tuple-element.82., ...), custom_call_target="tpu_custom_call" | custom-call | tf_op jit(solution)/shard_map/update/pallas_call | solution.py:1602

commit v4 on v3

--- a/solution.py
+++ b/solution.py
@@ -797,8 +797,8 @@
 ):
     def body(net, ins, outs, work):
         (
-            tokens_, cotangent_, query_, keyval_, output_, gateup_, down_, gains_, lengths_,
-            cosine_, sine_,
+            tokens_, cotangent_, query_, keyval_, output_, gateup_in, down_in, gains_, lengths_,
+            cosine_in, sine_in,
         ) = ins
         (
             residual_, tokens_here, normed_, raw_hbm, heads_hbm, attended_hbm, totals_hbm,
@@ -809,12 +809,18 @@
             gathered, normed, qkv_w, output_w, qkv_cast, output_cast, qkv_piece, output_piece,
             gains_row, gains_rows, lengths_mine, lengths_there, gate_cast, up_cast, down_cast,
             gate_piece, up_piece, cotangent_here, terms, raw_, heads_, attended_, totals_,
-            cosine_out, sine_out, landed, land,
+            cosine_out, sine_out, gateup_, down_, cosine_, sine_, landed, land,
         ) = work
         place = net.place
         units = Units(place)
         mine, theirs = place.core, 1 - place.core
 
+        loads = [
+            net.local(lambda source=source, target=target: (source, target))
+            for source, target in (
+                (gateup_in, gateup_), (down_in, down_), (cosine_in, cosine_), (sine_in, sine_),
+            )
+        ]
         qkv_cast[:, 0:256] = query_[...].astype(BF16)
         qkv_cast[:, 256:384] = keyval_[0].astype(BF16)
         qkv_cast[:, 384:512] = keyval_[1].astype(BF16)
@@ -841,6 +847,8 @@
         gains_steps = GainsGather(net, gains_row, gains_rows).steps()
         next(gains_steps)
 
+        for load in loads:
+            load.wait()
         halves = []
         for n, (cast, piece) in enumerate(((gate_cast, gate_piece), (up_cast, up_piece))):
             spot = own_half(128, mine)
@@ -1024,13 +1032,13 @@
 
     plans = (GainsGather,) + 4 * (PlaneGather,) + 2 * (RowsGather,) + (RowsSum,)
     return Kernel(
-        0, plans, 4, 6, 9, CORE_PARTNER + X_PARTNERS + FAR_X + PLANE_PARTNERS + TURN_PARTNERS
+        0, plans, 4, 6, 13, CORE_PARTNER + X_PARTNERS + FAR_X + PLANE_PARTNERS + TURN_PARTNERS
     )(
         body,
         [
             (tokens, VMEM), (cotangent, VMEM), (query, VMEM), (keyval, VMEM), (output, VMEM),
-            (gateup, VMEM), (down, VMEM), (gains, VMEM), (lengths, VMEM),
-            (cosine, VMEM), (sine, VMEM),
+            (gateup, HBM), (down, HBM), (gains, VMEM), (lengths, VMEM),
+            (cosine, HBM), (sine, HBM),
         ],
         [
             (shape((128, 2048), F32), VMEM),
@@ -1075,6 +1083,10 @@
             pltpu.VMEM((1024, 512), BF16),
             pltpu.VMEM((1024, 256), BF16),
             pltpu.VMEM((1024, 128), F32),
+            pltpu.VMEM((1024, 128), F32),
+            pltpu.VMEM((1024, 128), F32),
+            pltpu.VMEM((2, 128, 768), F32),
+            pltpu.VMEM((768, 128), F32),
             pltpu.VMEM((1024, 128), F32),
             pltpu.VMEM((1024, 128), F32),
         )

time: 235 us -> 234 us (level)
  no operation moved by 1% of the time
where the time goes in v4:
time: 234 us; the launch traced here: 233 us
  Pallas kernels  232 us (99%)
    pallas_call x2, Pallas kernels, __call__(): pl.pallas_call(kernel, out_shape=[shape for shape, _ in outs], in_specs=[...  227 us
    pallas_call x1, Pallas kernels, update(): pl.pallas_call(kernel, out_shape=outs, in_specs=[pl.BlockSpec(memory_spac...  5.66 us

profile of v4, /device:TPU:1, one launch (start us, length us, event | category | flops | bytes accessed | tf_op | source)
XLA Modules:
  0.0 233.2 jit_solution(17784449209160514180)
XLA Ops:
  0.7 83.9 %links_0.1 = (f32[128,2048]{1,0:T(8,128)}, bf16[128,2048]{1,0:T(8,128)(2,1)}, bf16[1024,2048]{1,0:T(8,128)(2,1)}, f32[1024,384]{1,0:T(8,128)}, bf16[1024,512]{1,...) custom-call(bf16[128,2048]{1,0:T(8,128)(2,1)} %refs_0_.1, ...), custom_call_target="tpu_custom_call" | custom-call | tf_op jit(solution)/shard_map/links_0/pallas_call | solution.py:644
  84.6 142.8 %links_1.1 = (bf16[128,2048]{1,0:T(8,128)(2,1)}, bf16[128,2048]{1,0:T(8,128)(2,1)}, bf16[128,512]{1,0:T(8,128)(2,1)}, bf16[256,128]{1,0:T(8,128)(2,1)}, bf16[128...) custom-call(f32[128,2048]{1,0:T(8,128)} %get-tuple-element.65.refs_0_, ...), custom_call_target="tpu_custom_call" | custom-call | tf_op jit(solution)/shard_map/links_1/pallas_call | solution.py:644
  227.4 5.7 %update.1 = (bf16[128,2048]{1,0:T(8,128)(2,1)}, bf16[128,2048]{1,0:T(8,128)(2,1)}, f32[128,256]{1,0:T(8,128)}, f32[2,128,128]{2,1,0:T(8,128)}, f32[256,128]{1,0:...) custom-call(bf16[128,2048]{1,0:T(8,128)(2,1)} %get-tuple-element.82., ...), custom_call_target="tpu_custom_call" | custom-call | tf_op jit(solution)/shard_map/update/pallas_call | solution.py:1614
